TPU v7x, 32 devices: a whole 2x2x4 slice. The times are simulated.
32 devices in a mesh: ctx: 8 (over z, x), fsdp: 4 (over y, core).
Axes of the slice: x: 2, y: 2, z: 4, core: 2. Of those that a mesh axis runs over, the one named last changes fastest.
Arguments:
- tokens: bfloat16 [4, 1024, 1024], P('fsdp', 'ctx'), may hold values from -6 to 6
- segments: int32 [4, 1024], P('fsdp'), may hold values from 0 to 2, as said below
- w_query: bfloat16 [1024, 512], P(('ctx', 'fsdp')), may hold values from -0.1875 to 0.1875
- key_value_weight: bfloat16 [1024, 256], P(('ctx', 'fsdp')), may hold values from -0.1875 to 0.1875
- w_attn_out: bfloat16 [512, 1024], P(None, ('ctx', 'fsdp')), may hold values from -1 to 1
- w_zgate: bfloat16 [1024, 1536], P(('ctx', 'fsdp')), may hold values from -0.1875 to 0.1875
- w_conv_in: bfloat16 [1024, 1792], P(('ctx', 'fsdp')), may hold values from -0.1875 to 0.1875
- w_step: bfloat16 [1024, 24], P(('ctx', 'fsdp')), may hold values from -0.1875 to 0.1875
- w_mix_out: bfloat16 [1536, 1024], P(None, ('ctx', 'fsdp')), may hold values from -0.15625 to 0.15625
- w_gate_up: bfloat16 [1024, 4096], P(('ctx', 'fsdp')), may hold values from -0.1875 to 0.1875
- w_down: bfloat16 [2048, 1024], P(None, ('ctx', 'fsdp')), may hold values from -0.125 to 0.125
- gain_in: float32 [1024], replicated, may hold values from 0.5 to 1.5
- gain_ffn: float32 [1024], replicated, may hold values from 0.5 to 1.5
- gain_mix: float32 [1536], replicated, may hold values from 0.5 to 1.5
- conv_weight: float32 [4, 1792], replicated, may hold values from -3 to 3
- conv_bias: float32 [1792], replicated, may hold values from -0.5 to 0.5
- step_bias: float32 [24], replicated, may hold values from -6 to 0
- decay_log: float32 [24], replicated, may hold values from -4.5 to -1
- skip_gain: float32 [24], replicated, may hold values from 0.5 to 1.5
- cotangent: bfloat16 [4, 1024, 1024], P('fsdp', 'ctx'), may hold values from -6 to 6
Outputs:
- output: bfloat16 [4, 1024, 1024], P('fsdp', 'ctx')
- grad_tokens: float32 [4, 1024, 1024], P('fsdp', 'ctx')
- grad_query: float32 [1024, 512], P(('ctx', 'fsdp'))
- grad_keyval: float32 [1024, 256], P(('ctx', 'fsdp'))
- grad_attn_out: float32 [512, 1024], P(None, ('ctx', 'fsdp'))
- grad_zgate: float32 [1024, 1536], P(('ctx', 'fsdp'))
- grad_conv_in: float32 [1024, 1792], P(('ctx', 'fsdp'))
- grad_step: float32 [1024, 24], P(('ctx', 'fsdp'))
- grad_mix_out: float32 [1536, 1024], P(None, ('ctx', 'fsdp'))
- grad_gate_up: float32 [1024, 4096], P(('ctx', 'fsdp'))
- grad_down: float32 [2048, 1024], P(None, ('ctx', 'fsdp'))
- grad_gain_in: float32 [1024], replicated
- grad_gain_ffn: float32 [1024], replicated
- grad_gain_mix: float32 [1536], replicated
- grad_conv_weight: float32 [4, 1792], replicated
- grad_conv_bias: float32 [1792], replicated
- grad_step_bias: float32 [24], replicated
- grad_decay_log: float32 [24], replicated
- grad_skip_gain: float32 [24], replicated
Inputs may be any that keep to these rules, and one draw needn't show every extreme that they name: `segments`: each row holds three documents numbered 0, 1, 2 in order: document 0 ends within the first 128 tokens of the row and document 2 begins within its last 128 tokens.
All inputs are finite; a program needn't handle non-finite values.
Results may differ from a plain program's by a relative error of at most 0.014.
Values may be sent and summed in bfloat16 or wider, within the bound.
A program may use at most 256 MiB of HBM per device.

v0:
```python
from functools import partial

import jax
import jax.numpy as jnp
from jax import lax
from jax.sharding import PartitionSpec as P

QUERY_HEADS = 8
KEY_VALUE_HEADS = 2
HEAD_SIZE = 64
MH = 24
MP = 64
NS = 128
FF = 2048
KC = 4
DI = 1536
XBC = 1792


norm_eps = 1e-05
rope_base = 100000000000.0
highest = lax.Precision.HIGHEST
score_masked = -1e30
key_block = 512


def from_behind(block, axis, distance):
    devices = range(lax.axis_size(axis))
    route = [(i - distance, i) for i in devices if i - distance in devices]
    return lax.ppermute(block, axis, route)


def entering(value, axis, combine, identity):
    count, index = (lax.axis_size(axis), lax.axis_index(axis))
    everything = jax.tree.map(
        lambda part, kind: lax.all_gather(part.astype(kind), axis),
        value,
        (jnp.bfloat16, jnp.bfloat16),
    )
    start = jax.tree.map(
        lambda part, zero: jnp.broadcast_to(jnp.asarray(zero, part.dtype), part.shape),
        value,
        identity,
    )

    def hop(k, before):
        reached = k < index
        new = combine(
            before, jax.tree.map(lambda part, own: part[k].astype(own.dtype), everything, value)
        )
        return jax.tree.map(lambda a, b: jnp.where(reached, a, b), new, before)

    return lax.fori_loop(0, count, hop, start)


def entering_2(value, axis, join, neutral):
    count = lax.axis_size(axis)
    place = lax.axis_index(axis)
    ahead = count - 1 - place
    gathered = jax.tree.map(
        lambda a, kind: lax.all_gather(a.astype(kind), axis),
        value,
        jax.tree.map(lambda a: jnp.bfloat16 if a.dtype == jnp.float32 else a.dtype, value),
    )
    state = jax.tree.map(lambda a, e: jnp.zeros_like(a) + jnp.asarray(e, a.dtype), value, neutral)

    def one(hop, state):
        source = count - 1 - hop
        return join(
            state,
            jax.tree.map(
                lambda a, own: lax.dynamic_index_in_dim(a, source, 0, False).astype(own.dtype),
                gathered,
                value,
            ),
        )

    return lax.fori_loop(0, ahead, one, state)


def rms_scale(values, gain):
    return values * lax.rsqrt(jnp.mean(values * values, axis=-1, keepdims=True) + norm_eps) * gain


def apply_rotation(values, cosine_table, sine_table):
    half = values.shape[-1] // 2
    turned = jnp.concatenate([-values[..., half:], values[..., :half]], axis=-1)
    return values * cosine_table + turned * sine_table


def angles(positions, width):
    freq = rope_base ** (-jnp.arange(0, width, 2).astype(jnp.float32) / width)
    phase = positions.astype(jnp.float32)[:, None] * freq[None, :]
    phase = jnp.concatenate([phase, phase], axis=-1)
    return (jnp.cos(phase), jnp.sin(phase))


def product(left, right):
    return jnp.dot(left, right, preferred_element_type=jnp.float32)


def product_left(left, right):
    return lax.dot_general(
        left, right, (((0,), (0,)), ((), ())), preferred_element_type=jnp.float32
    )


def product_right(left, right):
    return lax.dot_general(
        left, right, (((1,), (1,)), ((), ())), preferred_element_type=jnp.float32
    )


def block_scores(query_group_list, all_kv, block_index, seg_row, seg_own, positions, block_length):
    block_key_value = lax.dynamic_slice_in_dim(all_kv, block_index * block_length, block_length, 0)
    key_matrix = block_key_value[:, : KEY_VALUE_HEADS * HEAD_SIZE].reshape(
        block_length, KEY_VALUE_HEADS, HEAD_SIZE
    )
    raw_scores = jnp.einsum(
        "qkgd,skd->kgqs", query_group_list, key_matrix, preferred_element_type=jnp.float32
    ) * HEAD_SIZE ** (-0.5)
    key_pos = block_index * block_length + jnp.arange(block_length, dtype=jnp.int32)
    key_seg = lax.dynamic_slice_in_dim(seg_row, block_index * block_length, block_length, 0)
    allowed = (key_pos[None, :] <= positions[:, None]) & (key_seg[None, :] == seg_own[:, None])
    return (jnp.where(allowed[None, None], raw_scores, score_masked), block_key_value)


def attend_forward(query_batch, all_kv, seg_row, seg_own, positions, leading_block, required_flag):
    count_rows = query_batch.shape[0]
    block_length = min(key_block, all_kv.shape[0])
    group_width = QUERY_HEADS // KEY_VALUE_HEADS
    query_group_list = query_batch.reshape(count_rows, KEY_VALUE_HEADS, group_width, HEAD_SIZE)

    def first_pass(block_index, carry):
        running_max, running_sum = carry
        scores, block_key_value = block_scores(
            query_group_list, all_kv, block_index, seg_row, seg_own, positions, block_length
        )
        new_max = jnp.maximum(running_max, jnp.max(scores, axis=-1))
        running_sum = running_sum * jnp.exp(running_max - new_max) + jnp.sum(
            jnp.exp(scores - new_max[..., None]), axis=-1
        )
        return (new_max, running_sum)

    start_state = (
        jnp.full((KEY_VALUE_HEADS, group_width, count_rows), score_masked, jnp.float32),
        jnp.zeros((KEY_VALUE_HEADS, group_width, count_rows), jnp.float32),
    )
    running_max, running_sum = lax.fori_loop(leading_block, required_flag, first_pass, start_state)
    log_total = running_max + jnp.log(running_sum)

    def backward_sweep(block_index, weighted):
        scores, block_key_value = block_scores(
            query_group_list, all_kv, block_index, seg_row, seg_own, positions, block_length
        )
        weights = jnp.exp(scores - log_total[..., None]).astype(jnp.bfloat16)
        value_matrix = block_key_value[:, KEY_VALUE_HEADS * HEAD_SIZE :].reshape(
            block_length, KEY_VALUE_HEADS, HEAD_SIZE
        )
        return weighted + jnp.einsum(
            "kgqs,skd->qkgd", weights, value_matrix, preferred_element_type=jnp.float32
        )

    weighted = lax.fori_loop(
        leading_block,
        required_flag,
        backward_sweep,
        jnp.zeros((count_rows, KEY_VALUE_HEADS, group_width, HEAD_SIZE), jnp.float32),
    )
    return (weighted.reshape(count_rows, QUERY_HEADS * HEAD_SIZE), log_total)


def attend_backward(
    query_batch,
    all_kv,
    gradient_batch,
    attention_result,
    log_total,
    seg_row,
    seg_own,
    positions,
    leading_block,
    required_flag,
):
    count_rows = query_batch.shape[0]
    group_width = QUERY_HEADS // KEY_VALUE_HEADS
    token_length = all_kv.shape[0]
    block_length = min(key_block, token_length)
    query_group_list = query_batch.reshape(count_rows, KEY_VALUE_HEADS, group_width, HEAD_SIZE)
    gradient_groups = gradient_batch.reshape(count_rows, KEY_VALUE_HEADS, group_width, HEAD_SIZE)
    row_dot = jnp.einsum(
        "qkgd,qkgd->kgq",
        gradient_groups.astype(jnp.float32),
        attention_result.reshape(count_rows, KEY_VALUE_HEADS, group_width, HEAD_SIZE),
    )

    def one_block(block_index, carry):
        grad_query, grad_kv = carry
        scores, block_key_value = block_scores(
            query_group_list, all_kv, block_index, seg_row, seg_own, positions, block_length
        )
        weights = jnp.exp(scores - log_total[..., None])
        key_matrix = block_key_value[:, : KEY_VALUE_HEADS * HEAD_SIZE].reshape(
            block_length, KEY_VALUE_HEADS, HEAD_SIZE
        )
        value_matrix = block_key_value[:, KEY_VALUE_HEADS * HEAD_SIZE :].reshape(
            block_length, KEY_VALUE_HEADS, HEAD_SIZE
        )
        grad_weights = jnp.einsum(
            "qkgd,skd->kgqs", gradient_groups, value_matrix, preferred_element_type=jnp.float32
        )
        grad_scores = (weights * (grad_weights - row_dot[..., None])).astype(jnp.bfloat16)
        grad_query = grad_query + jnp.einsum(
            "kgqs,skd->qkgd", grad_scores, key_matrix, preferred_element_type=jnp.float32
        ) * HEAD_SIZE ** (-0.5)
        gradient_key_rows = jnp.einsum(
            "kgqs,qkgd->skd", grad_scores, query_group_list, preferred_element_type=jnp.float32
        ) * HEAD_SIZE ** (-0.5)
        gradient_value_rows = jnp.einsum(
            "kgqs,qkgd->skd",
            weights.astype(jnp.bfloat16),
            gradient_groups,
            preferred_element_type=jnp.float32,
        )
        update = jnp.concatenate(
            [
                gradient_key_rows.reshape(block_length, KEY_VALUE_HEADS * HEAD_SIZE),
                gradient_value_rows.reshape(block_length, KEY_VALUE_HEADS * HEAD_SIZE),
            ],
            axis=1,
        )
        grad_kv = lax.dynamic_update_slice_in_dim(grad_kv, update, block_index * block_length, 0)
        return (grad_query, grad_kv)

    start_state = (
        jnp.zeros((count_rows, KEY_VALUE_HEADS, group_width, HEAD_SIZE), jnp.float32),
        jnp.zeros((token_length, 2 * KEY_VALUE_HEADS * HEAD_SIZE), jnp.float32),
    )
    grad_query, grad_kv = lax.fori_loop(leading_block, required_flag, one_block, start_state)
    return (grad_query.reshape(count_rows, QUERY_HEADS, HEAD_SIZE), grad_kv)


def conv_mix(extended, step_raw, conv_weight, conv_bias, step_bias, decay_log, seg_ext, seg_own):
    count_rows = step_raw.shape[0]
    conv_sum = conv_bias + jnp.zeros((count_rows, XBC), jnp.float32)
    for tap in range(KC):
        same = seg_ext[tap : tap + count_rows] == seg_own
        conv_sum = conv_sum + conv_weight[tap] * jnp.where(
            same[:, None], extended[tap : tap + count_rows], 0.0
        )
    activated = jax.nn.silu(conv_sum)
    step_size = jax.nn.softplus(step_raw + step_bias)
    log_decay = jnp.cumsum(step_size * -jnp.exp(decay_log), axis=0)
    return (activated, step_size, log_decay)


def split_inputs(activated):
    count_rows = activated.shape[0]
    return (
        activated[:, :DI].reshape(count_rows, MH, MP),
        activated[:, DI : DI + NS],
        activated[:, DI + NS :],
    )


def compute_end_state(activated, step_size, log_decay, seg_own, seg_before):
    mix_input, b_proj, c_proj = split_inputs(activated)
    last_segment = seg_own[-1]
    tail_weight = (
        jnp.exp(log_decay[-1][None, :] - log_decay) * (seg_own == last_segment)[:, None] * step_size
    )
    state_local = jnp.einsum("sh,shp,sn->hpn", tail_weight, mix_input, b_proj, precision=highest)
    end_decay = jnp.exp(log_decay[-1]) * (last_segment == seg_before)
    return (end_decay, state_local)


def mix_output(
    activated, step_size, log_decay, gate_values, skip_gain, gain_mix, state_in, seg_own, seg_before
):
    count_rows = activated.shape[0]
    mix_input, b_proj, c_proj = split_inputs(activated)
    places = jnp.arange(count_rows)
    allowed = (places[None, :] <= places[:, None]) & (seg_own[None, :] == seg_own[:, None])
    spread = jnp.exp(
        jnp.where(allowed[:, :, None], log_decay[:, None, :] - log_decay[None, :, :], -10000.0)
    )
    inner = jnp.dot(c_proj, b_proj.T, precision=highest)
    mixing = spread * inner[:, :, None] * step_size[None, :, :]
    y_local = jnp.einsum("tsh,shp->thp", mixing, mix_input, precision=highest)
    coef_in = jnp.exp(log_decay) * (seg_own == seg_before)[:, None]
    carried = jnp.einsum("tn,hpn->thp", c_proj, state_in, precision=highest)
    y_total = y_local + coef_in[:, :, None] * carried + skip_gain[None, :, None] * mix_input
    gated = y_total.reshape(count_rows, DI) * jax.nn.silu(gate_values)
    return rms_scale(gated, gain_mix)


def chain(earlier, later):
    return (earlier[0] * later[0], later[0][:, None, None] * earlier[1] + later[1])


def gate_product(gate_up):
    return jax.nn.silu(gate_up[:, :FF]) * gate_up[:, FF:]


def per_device(
    tokens,
    segments,
    w_query,
    key_value_weight,
    w_attn_out,
    w_zgate,
    w_conv_in,
    w_step,
    w_mix_out,
    w_gate_up,
    w_down,
    gain_in,
    gain_ffn,
    gain_mix,
    conv_weight,
    conv_bias,
    step_bias,
    decay_log,
    skip_gain,
    cotangent,
):
    count_rows = tokens.shape[1]
    block_length = min(key_block, count_rows * lax.axis_size("ctx"))
    row_start = lax.axis_index("ctx") * count_rows
    seg_row = segments[0]
    seg_own = lax.dynamic_slice_in_dim(seg_row, row_start, count_rows, 0)
    seg_pad = jnp.concatenate([jnp.full((KC - 1,), -1, jnp.int32), seg_row])
    seg_ext = lax.dynamic_slice_in_dim(seg_pad, row_start, count_rows + KC - 1, 0)
    seg_before = seg_ext[KC - 2]
    positions = row_start + jnp.arange(count_rows, dtype=jnp.int32)
    leading_block = jnp.searchsorted(seg_row, seg_own[0]) // block_length
    required_flag = positions[-1] // block_length + 1
    (
        query_full,
        keyval_full,
        attn_out_full,
        zgate_full,
        conv_in_full,
        step_full,
        mix_out_full,
        gate_up_full,
        down_full,
    ) = (
        lax.all_gather(w_query, ("ctx", "fsdp"), axis=0, tiled=True),
        lax.all_gather(key_value_weight, ("ctx", "fsdp"), axis=0, tiled=True),
        lax.all_gather(w_attn_out, ("ctx", "fsdp"), axis=1, tiled=True),
        lax.all_gather(w_zgate, ("ctx", "fsdp"), axis=0, tiled=True),
        lax.all_gather(w_conv_in, ("ctx", "fsdp"), axis=0, tiled=True),
        lax.all_gather(w_step, ("ctx", "fsdp"), axis=0, tiled=True),
        lax.all_gather(w_mix_out, ("ctx", "fsdp"), axis=1, tiled=True),
        lax.all_gather(w_gate_up, ("ctx", "fsdp"), axis=0, tiled=True),
        lax.all_gather(w_down, ("ctx", "fsdp"), axis=1, tiled=True),
    )
    x_rows = tokens[0].astype(jnp.float32)
    normed, pull_in = jax.vjp(rms_scale, x_rows, gain_in)
    normed_b = normed.astype(jnp.bfloat16)
    cosine_table, sine_table = angles(positions, HEAD_SIZE)
    query_rot = apply_rotation(
        product(normed_b, query_full).reshape(count_rows, QUERY_HEADS, HEAD_SIZE),
        cosine_table[:, None],
        sine_table[:, None],
    )
    query_batch = query_rot.astype(jnp.bfloat16)
    key_value_pair = product(normed_b, keyval_full)
    key_rotated = apply_rotation(
        key_value_pair[:, : KEY_VALUE_HEADS * HEAD_SIZE].reshape(
            count_rows, KEY_VALUE_HEADS, HEAD_SIZE
        ),
        cosine_table[:, None],
        sine_table[:, None],
    )
    keyval_b = jnp.concatenate(
        [
            key_rotated.reshape(count_rows, KEY_VALUE_HEADS * HEAD_SIZE),
            key_value_pair[:, KEY_VALUE_HEADS * HEAD_SIZE :],
        ],
        axis=1,
    ).astype(jnp.bfloat16)
    all_kv = lax.all_gather(keyval_b, "ctx", axis=0, tiled=True)
    attention_result, log_total = attend_forward(
        query_batch, all_kv, seg_row, seg_own, positions, leading_block, required_flag
    )
    attended_b = attention_result.astype(jnp.bfloat16)
    attn_out = product(attended_b, attn_out_full)
    gate_values = product(normed_b, zgate_full)
    conv_in_b = product(normed_b, conv_in_full).astype(jnp.bfloat16)
    step_raw = product(normed_b, step_full)
    before_rows = from_behind(conv_in_b[count_rows - (KC - 1) :], "ctx", 1)
    extended = jnp.concatenate([before_rows, conv_in_b], axis=0).astype(jnp.float32)
    (activated, step_size, log_decay), pull_pre = jax.vjp(
        partial(conv_mix, seg_ext=seg_ext, seg_own=seg_own),
        extended,
        step_raw,
        conv_weight,
        conv_bias,
        step_bias,
        decay_log,
    )
    (end_decay, state_local), pull_state = jax.vjp(
        partial(compute_end_state, seg_own=seg_own, seg_before=seg_before),
        activated,
        step_size,
        log_decay,
    )
    identity = (jnp.ones_like(end_decay), jnp.zeros_like(state_local))
    state_in = entering((end_decay, state_local), "ctx", chain, identity)[1]
    mixed, pull_mix = jax.vjp(
        partial(mix_output, seg_own=seg_own, seg_before=seg_before),
        activated,
        step_size,
        log_decay,
        gate_values,
        skip_gain,
        gain_mix,
        state_in,
    )
    mixed_b = mixed.astype(jnp.bfloat16)
    mix_out = product(mixed_b, mix_out_full)
    hidden = x_rows + attn_out + mix_out
    hnorm, pull_ffn = jax.vjp(rms_scale, hidden, gain_ffn)
    hnorm_b = hnorm.astype(jnp.bfloat16)
    gate_up = product(hnorm_b, gate_up_full)
    ffn_act, pull_act = jax.vjp(gate_product, gate_up)
    ffn_act_b = ffn_act.astype(jnp.bfloat16)
    result = hidden + product(ffn_act_b, down_full)
    (
        query_full,
        keyval_full,
        attn_out_full,
        zgate_full,
        conv_in_full,
        step_full,
        mix_out_full,
        gate_up_full,
        down_full,
    ) = (
        lax.all_gather(w_query, ("ctx", "fsdp"), axis=0, tiled=True),
        lax.all_gather(key_value_weight, ("ctx", "fsdp"), axis=0, tiled=True),
        lax.all_gather(w_attn_out, ("ctx", "fsdp"), axis=1, tiled=True),
        lax.all_gather(w_zgate, ("ctx", "fsdp"), axis=0, tiled=True),
        lax.all_gather(w_conv_in, ("ctx", "fsdp"), axis=0, tiled=True),
        lax.all_gather(w_step, ("ctx", "fsdp"), axis=0, tiled=True),
        lax.all_gather(w_mix_out, ("ctx", "fsdp"), axis=1, tiled=True),
        lax.all_gather(w_gate_up, ("ctx", "fsdp"), axis=0, tiled=True),
        lax.all_gather(w_down, ("ctx", "fsdp"), axis=1, tiled=True),
    )
    grad_result = cotangent[0].astype(jnp.float32)
    grad_result_b = grad_result.astype(jnp.bfloat16)
    grad_down_full = product_left(ffn_act_b, grad_result_b)
    (grad_gate_up_rows,) = pull_act(product_right(grad_result_b, down_full))
    grad_gate_up_b = grad_gate_up_rows.astype(jnp.bfloat16)
    grad_gate_up_full = product_left(hnorm_b, grad_gate_up_b)
    grad_hidden_norm, grad_gain_ffn = pull_ffn(product_right(grad_gate_up_b, gate_up_full))
    grad_hidden = grad_result + grad_hidden_norm
    grad_hidden_b = grad_hidden.astype(jnp.bfloat16)
    grad_attn_out_full = product_left(attended_b, grad_hidden_b)
    grad_mix_out_full = product_left(mixed_b, grad_hidden_b)
    grad_attn_out, grad_mix_out, grad_gate_up, grad_down = (
        lax.psum_scatter(grad_attn_out_full, ("ctx", "fsdp"), scatter_dimension=1, tiled=True),
        lax.psum_scatter(grad_mix_out_full, ("ctx", "fsdp"), scatter_dimension=1, tiled=True),
        lax.psum_scatter(grad_gate_up_full, ("ctx", "fsdp"), scatter_dimension=0, tiled=True),
        lax.psum_scatter(grad_down_full, ("ctx", "fsdp"), scatter_dimension=1, tiled=True),
    )
    grad_attended_b = product_right(grad_hidden_b, attn_out_full).astype(jnp.bfloat16)
    grad_mixed = product_right(grad_hidden_b, mix_out_full)
    grad_query_rot, grad_kv_all = attend_backward(
        query_batch,
        all_kv,
        grad_attended_b,
        attention_result,
        log_total,
        seg_row,
        seg_own,
        positions,
        leading_block,
        required_flag,
    )
    gradient_key_value_rows = lax.psum_scatter(grad_kv_all, "ctx", scatter_dimension=0, tiled=True)
    grad_query_b = (
        apply_rotation(grad_query_rot, cosine_table[:, None], -sine_table[:, None])
        .reshape(count_rows, QUERY_HEADS * HEAD_SIZE)
        .astype(jnp.bfloat16)
    )
    gradient_key_prerotation = apply_rotation(
        gradient_key_value_rows[:, : KEY_VALUE_HEADS * HEAD_SIZE].reshape(
            count_rows, KEY_VALUE_HEADS, HEAD_SIZE
        ),
        cosine_table[:, None],
        -sine_table[:, None],
    )
    grad_keyval_b = jnp.concatenate(
        [
            gradient_key_prerotation.reshape(count_rows, KEY_VALUE_HEADS * HEAD_SIZE),
            gradient_key_value_rows[:, KEY_VALUE_HEADS * HEAD_SIZE :],
        ],
        axis=1,
    ).astype(jnp.bfloat16)
    (
        grad_act_mix,
        grad_step_mix,
        grad_decay_mix,
        grad_gate_values,
        grad_skip_gain,
        grad_gain_mix,
        grad_state_in,
    ) = pull_mix(grad_mixed)
    later_grads = entering_2((end_decay, grad_state_in), "ctx", chain, identity)[1]
    grad_end_decay = jnp.sum(later_grads * state_in, axis=(1, 2))
    grad_act_state, grad_step_state, grad_decay_state = pull_state((grad_end_decay, later_grads))
    (
        grad_extended,
        grad_step_raw,
        grad_conv_weight,
        grad_conv_bias,
        grad_step_bias,
        grad_decay_log,
    ) = pull_pre(
        (
            grad_act_mix + grad_act_state,
            grad_step_mix + grad_step_state,
            grad_decay_mix + grad_decay_state,
        )
    )
    from_next = from_behind(grad_extended[: KC - 1], "ctx", -1)
    grad_conv_rows = grad_extended[KC - 1 :].at[count_rows - (KC - 1) :].add(from_next)
    grad_conv_b = grad_conv_rows.astype(jnp.bfloat16)
    grad_gate_b = grad_gate_values.astype(jnp.bfloat16)
    grad_step_b = grad_step_raw.astype(jnp.bfloat16)
    grad_normed = (
        product_right(grad_query_b, query_full)
        + product_right(grad_keyval_b, keyval_full)
        + product_right(grad_gate_b, zgate_full)
        + product_right(grad_conv_b, conv_in_full)
        + product_right(grad_step_b, step_full)
    )
    grad_x_norm, grad_gain_in = pull_in(grad_normed)
    grad_tokens = grad_hidden + grad_x_norm
    grad_query, grad_keyval, grad_zgate, grad_conv_in, grad_step = (
        lax.psum_scatter(
            product_left(normed_b, grad_query_b), ("ctx", "fsdp"), scatter_dimension=0, tiled=True
        ),
        lax.psum_scatter(
            product_left(normed_b, grad_keyval_b), ("ctx", "fsdp"), scatter_dimension=0, tiled=True
        ),
        lax.psum_scatter(
            product_left(normed_b, grad_gate_b), ("ctx", "fsdp"), scatter_dimension=0, tiled=True
        ),
        lax.psum_scatter(
            product_left(normed_b, grad_conv_b), ("ctx", "fsdp"), scatter_dimension=0, tiled=True
        ),
        lax.psum_scatter(
            product_left(normed_b, grad_step_b), ("ctx", "fsdp"), scatter_dimension=0, tiled=True
        ),
    )
    (
        sum_gain_in,
        sum_gain_ffn,
        sum_gain_mix,
        sum_conv_weight,
        sum_conv_bias,
        sum_step_bias,
        sum_decay_log,
        sum_skip_gain,
    ) = lax.psum(
        (
            grad_gain_in,
            grad_gain_ffn,
            grad_gain_mix,
            grad_conv_weight,
            grad_conv_bias,
            grad_step_bias,
            grad_decay_log,
            grad_skip_gain,
        ),
        ("ctx", "fsdp"),
    )
    return (
        result[None].astype(jnp.bfloat16),
        grad_tokens[None],
        grad_query,
        grad_keyval,
        grad_attn_out,
        grad_zgate,
        grad_conv_in,
        grad_step,
        grad_mix_out,
        grad_gate_up,
        grad_down,
        sum_gain_in,
        sum_gain_ffn,
        sum_gain_mix,
        sum_conv_weight,
        sum_conv_bias,
        sum_step_bias,
        sum_decay_log,
        sum_skip_gain,
    )


def solution(mesh):
    in_specs = (
        P("fsdp", "ctx", None),
        P("fsdp", None),
        P(("ctx", "fsdp"), None),
        P(("ctx", "fsdp"), None),
        P(None, ("ctx", "fsdp")),
        P(("ctx", "fsdp"), None),
        P(("ctx", "fsdp"), None),
        P(("ctx", "fsdp"), None),
        P(None, ("ctx", "fsdp")),
        P(("ctx", "fsdp"), None),
        P(None, ("ctx", "fsdp")),
        P(),
        P(),
        P(),
        P(),
        P(),
        P(),
        P(),
        P(),
        P("fsdp", "ctx", None),
    )
    out_specs = (
        P("fsdp", "ctx", None),
        P("fsdp", "ctx", None),
        P(("ctx", "fsdp"), None),
        P(("ctx", "fsdp"), None),
        P(None, ("ctx", "fsdp")),
        P(("ctx", "fsdp"), None),
        P(("ctx", "fsdp"), None),
        P(("ctx", "fsdp"), None),
        P(None, ("ctx", "fsdp")),
        P(("ctx", "fsdp"), None),
        P(None, ("ctx", "fsdp")),
        P(),
        P(),
        P(),
        P(),
        P(),
        P(),
        P(),
        P(),
    )
    return jax.shard_map(
        per_device, mesh=mesh, in_specs=in_specs, out_specs=out_specs, check_vma=False
    )
```

profile of v0, /device:TPU:0, one launch (start us, length us, event | category | flops | bytes accessed | tf_op | source)
XLA Modules:
  0.0 1953.5 jit_solution(7032063366977316112)
XLA Ops:
  11.9 44.2 %all-gather.2 = bf16[32,32,24]{1,2,0:T(8,128)(2,1)S(1)} all-gather(bf16[1,32,24]{1,2,0:T(8,128)(2,1)} %bitcast.452), channel_id=1, replica_groups=mesh['ctx'=8,'fsdp'=4] {'ctx','fsdp'}, dimensions={0}, use_global_device_ids=true | all-gather | bytes 50688 | tf_op jit(solution)/shard_map/all_gather | solution.py:354
  61.6 12.6 all-gather.18.cloned.1.call-done
  74.2 2.7 convolution_convert_fusion
  77.0 3.3 collective-permute-start
  91.8 21.0 %while.86 = (s32[]{:T(128)}, u32[]{:T(128)}, u32[]{:T(128)}, s32[1024]{0:T(1024)S(1)}, s32[]{:T(128)}, /*index=5*/s32[]{:T(128)}, u32[]{:T(128)}) while((s32[]{:T(128)}, u32[]{:T(128)}, u32[]{:T(128)}, s32[1024]{0:T(1024)S(1)}, s32[]{:T(128)}, /*index=5*/s32[]{:T(128)}, u32[]{:T(128)}) %tuple.282), condition=%wide.region_1.2_spmd, body=%wide.region_0.1_spmd.sunk | while | flops 8 | bytes 160 | solution.py:336
  116.0 42.0 %all_gather.57 = bf16[1024,256]{1,0:T(8,128)(2,1)S(1)} all-gather(bf16[32,256]{1,0:T(8,128)(2,1)S(1)} %copy-done.72), channel_id=1, replica_groups=mesh['ctx'=8,'fsdp'=4] {'ctx','fsdp'}, dimensions={0}, use_global_device_ids=true | all-gather | bytes 540672 | tf_op jit(solution)/shard_map/all_gather | solution.py:350
  159.3 16.2 all-gather.3
  177.9 32.1 %all_gather.58 = bf16[1024,256]{1,0:T(8,128)(2,1)S(1)} all-gather(bf16[128,256]{1,0:T(8,128)(2,1)S(1)} %pad_maximum_fusion.1), channel_id=1, replica_groups=mesh['ctx'=8,'fsdp'=4] {'ctx'}, dimensions={0}, use_global_device_ids=true | all-gather | bytes 589824 | tf_op jit(solution)/shard_map/all_gather | solution.py:384
  221.4 27.2 %all-gather.28.cloned.1.call-done = bf16[192,64,128]{2,1,0:T(8,128)(2,1)} async-done(((bf16[24,64,128]{2,1,0:T(8,128)(2,1)}), bf16[192,64,128]{2,1,0:T(8,128)(2,1)}) %all-gather.28.cloned.1.call-update) | async-done | bytes 3145744 | tf_op jit(solution)/shard_map/all_gather | solution.py:36
  248.7 15.2 while.91
  266.5 5.5 fusion.48
  274.3 34.8 %all-gather.20.cloned.1.call-done = bf16[1024,1536]{1,0:T(8,128)(2,1)} async-done(((bf16[32,1536]{1,0:T(8,128)(2,1)}), bf16[1024,1536]{1,0:T(8,128)(2,1)}) %all-gather.20.cloned.1.call-update) | async-done | bytes 3145744 | tf_op jit(solution)/shard_map/all_gather | solution.py:352
  309.1 3.9 multiply_reduce_fusion.11
  313.0 56.7 %all-gather.22.cloned.1.call-done = bf16[1536,1024]{0,1:T(8,128)(2,1)} async-done(((bf16[1536,32]{0,1:T(8,128)(2,1)}), bf16[1536,1024]{0,1:T(8,128)(2,1)}) %all-gather.22.cloned.1.call-update) | async-done | bytes 3145744 | tf_op jit(solution)/shard_map/all_gather | solution.py:355
  369.7 3.5 multiply_reduce_fusion.14
  373.2 75.8 %all-gather.24.cloned.1.call-done = bf16[1024,4096]{1,0:T(8,128)(2,1)} async-done(((bf16[32,4096]{1,0:T(8,128)(2,1)}), bf16[1024,4096]{1,0:T(8,128)(2,1)}) %all-gather.24.cloned.1.call-update) | async-done | bytes 8388624 | tf_op jit(solution)/shard_map/all_gather | solution.py:356
  449.0 6.1 fusion.166
  455.1 57.4 %all-gather.26.cloned.1.call-done = bf16[2048,1024]{0,1:T(8,128)(2,1)} async-done(((bf16[2048,32]{0,1:T(8,128)(2,1)}), bf16[2048,1024]{0,1:T(8,128)(2,1)}) %all-gather.26.cloned.1.call-update) | async-done | bytes 4194320 | tf_op jit(solution)/shard_map/all_gather | solution.py:357
  512.5 5.0 fusion.120
  517.9 3.5 multiply_reduce_fusion.12
  526.2 6.5 while.90
  532.9 3.6 multiply_reduce_fusion.7
  541.2 2.7 convolution_convert_fusion.1
  546.1 5.5 fusion.58
  551.6 50.2 %reduce-scatter.13.cloned.1.call-done = f32[128,256]{0,1:T(8,128)} async-done(((f32[1024,256]{0,1:T(8,128)}), f32[128,256]{0,1:T(8,128)}) %reduce-scatter.13.cloned.1.call-update) | async-done | bytes 131088 | tf_op jit(solution)/shard_map/reduce_scatter | solution.py:483
  604.3 59.8 %all-gather.30.cloned.1.call-done = bf16[192,64,128]{2,1,0:T(8,128)(2,1)} async-done(((bf16[24,64,128]{2,1,0:T(8,128)(2,1)}), bf16[192,64,128]{2,1,0:T(8,128)(2,1)}) %all-gather.30.cloned.1.call-update) | async-done | bytes 3145744 | tf_op jit(solution)/shard_map/all_gather | solution.py:61
  664.2 13.5 while.87
  677.7 2.9 broadcast_multiply_fusion
  701.6 2.8 fusion.187
  704.4 4.8 fusion.167
  709.3 4.7 fusion.171
  714.1 5.7 fusion.106
  720.7 4.1 fusion.42
  736.4 3.1 multiply_reduce_fusion.4
  742.1 3.8 collective-permute-done.1
  746.2 4.1 fusion.114
  751.0 9.8 fusion.117
  763.5 4.6 fusion.53
  772.8 38.5 %all-reduce.18 = (f32[1024]{0:T(1024)}, f32[1024]{0:T(1024)}, f32[1536]{0:T(1024)}, f32[4,1792]{1,0:T(4,128)}, f32[1792]{0:T(1024)}, /*index=5*/f32[24]{0:T(128)}, f32[24]{0:T(128)}, f32[24]{0:T(128)}) all-reduce(f32[1024]{0:T(1024)S(1)} %get-tuple-element.666, ...), channel_id=1, replica_groups=mesh['ctx'=8,'fsdp'=4] {'ctx','fsdp'}, use_global_device_ids=true, to_apply=%region_40.41 | all-reduce | flops 12616 | bytes 100928 | tf_op jit(solution)/shard_map/psum | solution.py:569
  812.4 14.2 reduce-scatter.31.cloned.1.call-done
  828.0 132.0 %reduce-scatter.17.cloned.1.call-done = f32[32,256]{1,0:T(8,128)} async-done(((f32[1024,256]{1,0:T(8,128)}), f32[32,256]{1,0:T(8,128)}) %reduce-scatter.17.cloned.1.call-update) | async-done | bytes 32784 | tf_op jit(solution)/shard_map/reduce_scatter | solution.py:547
  960.1 135.5 %reduce-scatter.15.cloned.1.call-done = f32[32,512]{1,0:T(8,128)} async-done(((f32[1024,512]{1,0:T(8,128)}), f32[32,512]{1,0:T(8,128)}) %reduce-scatter.15.cloned.1.call-update) | async-done | bytes 65552 | tf_op jit(solution)/shard_map/reduce_scatter | solution.py:544
  1095.5 135.2 %reduce-scatter.19.cloned.1.call-done = f32[512,32]{0,1:T(8,128)} async-done(((f32[512,1024]{0,1:T(8,128)}), f32[512,32]{0,1:T(8,128)}) %reduce-scatter.19.cloned.1.call-update) | async-done | bytes 65552 | tf_op jit(solution)/shard_map/reduce_scatter | solution.py:464
  1230.8 117.5 %reduce-scatter.25.cloned.1.call-done = f32[1536,32]{0,1:T(8,128)} async-done(((f32[1536,1024]{0,1:T(8,128)}), f32[1536,32]{0,1:T(8,128)}) %reduce-scatter.25.cloned.1.call-update) | async-done | bytes 196624 | tf_op jit(solution)/shard_map/reduce_scatter | solution.py:465
  1348.3 119.7 %reduce-scatter.21.cloned.1.call-done = f32[32,1536]{1,0:T(8,128)} async-done(((f32[1024,1536]{1,0:T(8,128)}), f32[32,1536]{1,0:T(8,128)}) %reduce-scatter.21.cloned.1.call-update) | async-done | bytes 196624 | tf_op jit(solution)/shard_map/reduce_scatter | solution.py:550
  1468.0 151.1 %reduce-scatter.29.cloned.1.call-done = f32[2048,32]{0,1:T(8,128)} async-done(((f32[2048,1024]{0,1:T(8,128)}), f32[2048,32]{0,1:T(8,128)}) %reduce-scatter.29.cloned.1.call-update) | async-done | bytes 262160 | tf_op jit(solution)/shard_map/reduce_scatter | solution.py:467
  1619.1 145.6 %reduce-scatter.23.cloned.1.call-done = f32[32,1792]{1,0:T(8,128)} async-done(((f32[1024,1792]{1,0:T(8,128)}), f32[32,1792]{1,0:T(8,128)}) %reduce-scatter.23.cloned.1.call-update) | async-done | bytes 229392 | tf_op jit(solution)/shard_map/reduce_scatter | solution.py:553
  1764.7 181.9 %reduce-scatter.27.cloned.1.call-done = f32[32,4096]{1,0:T(8,128)} async-done(((f32[1024,4096]{1,0:T(8,128)}), f32[32,4096]{1,0:T(8,128)}) %reduce-scatter.27.cloned.1.call-update) | async-done | bytes 524304 | tf_op jit(solution)/shard_map/reduce_scatter | solution.py:466
  (458 shorter events, 145.1 us)
Async XLA Ops:
  7.2 51.7 %copy-start.36 = (s32[1,1024]{1,0:T(1,128)S(1)}, s32[1,1024]{1,0:T(1,128)}, u32[]{:S(2)}) copy-start(s32[1,1024]{1,0:T(1,128)} %param.35) | copy-start | bytes 12292
  7.2 67.0 %copy-start.1 = (bf16[1,128,1024]{2,1,0:T(8,128)(2,1)S(1)}, bf16[1,128,1024]{2,1,0:T(8,128)(2,1)}, u32[]{:S(2)}) copy-start(bf16[1,128,1024]{2,1,0:T(8,128)(2,1)} %param.34) | copy-start | bytes 786436
  7.2 67.0 %copy-start.32 = (f32[1024]{0:T(1024)S(1)}, f32[1024]{0:T(1024)}, u32[]{:S(2)}) copy-start(f32[1024]{0:T(1024)} %param.45) | copy-start | bytes 12292
  7.2 67.0 %all-gather.18.cloned.1.call-start = ((), (), s32[]{:S(2)}) async-start(), calls=%async_computation.12 | async-start | bytes 3784704 | tf_op jit(solution)/shard_map/all_gather | solution.py:353
  8.0 202.3 %all-gather.14.cloned.1.call-start = ((), (), s32[]{:S(2)}) async-start(), calls=%async_computation.10 | async-start | bytes 1081344 | tf_op jit(solution)/shard_map/all_gather | solution.py:349
  8.7 208.9 %all-gather.16.cloned.1.call-start = ((), (), s32[]{:S(2)}) async-start(), calls=%async_computation.11 | async-start | bytes 1081344 | tf_op jit(solution)/shard_map/all_gather | solution.py:351
  9.4 239.2 %all-gather.28.cloned.1.call-start = ((), (), s32[]{:S(2)}) async-start(), calls=%async_computation.26 | async-start | bytes 3538944 | tf_op jit(solution)/shard_map/all_gather | solution.py:36
  11.9 47.0 %copy-start.101 = (f32[128]{0:T(128)}, f32[128]{0:T(128)S(1)}, u32[]{:S(2)}) copy-start(f32[128]{0:T(128)S(1)} %fusion.90) | copy-start | bytes 1540
  60.9 20.9 %copy-start.89 = (pred[128]{0:T(512)(128)(4,1)}, pred[128]{0:T(512)(128)(4,1)S(1)}, u32[]{:S(2)}) copy-start(pred[128]{0:T(512)(128)(4,1)S(1)} %get-tuple-element.815) | copy-start | bytes 388
  60.9 21.0 %copy-start.91 = (pred[128]{0:T(512)(128)(4,1)}, pred[128]{0:T(512)(128)(4,1)S(1)}, u32[]{:S(2)}) copy-start(pred[128]{0:T(512)(128)(4,1)S(1)} %get-tuple-element.816) | copy-start | bytes 388
  60.9 21.0 %copy-start.93 = (pred[128]{0:T(512)(128)(4,1)}, pred[128]{0:T(512)(128)(4,1)S(1)}, u32[]{:S(2)}) copy-start(pred[128]{0:T(512)(128)(4,1)S(1)} %get-tuple-element.817) | copy-start | bytes 388
  77.0 4.7 collective-permute-start
  84.8 31.2 %copy-start.72 = (bf16[32,256]{1,0:T(8,128)(2,1)S(1)}, bf16[32,256]{1,0:T(8,128)(2,1)}, u32[]{:S(2)}) copy-start(bf16[32,256]{1,0:T(8,128)(2,1)} %param.37) | copy-start | bytes 49156
  87.7 221.3 %all-gather.20.cloned.1.call-start = ((), (), s32[]{:S(2)}) async-start(), calls=%async_computation.13 | async-start | bytes 3244032 | tf_op jit(solution)/shard_map/all_gather | solution.py:352
  88.3 281.4 %all-gather.22.cloned.1.call-start = ((), (), s32[]{:S(2)}) async-start(), calls=%async_computation.14 | async-start | bytes 3244032 | tf_op jit(solution)/shard_map/all_gather | solution.py:355
  88.9 360.1 %all-gather.24.cloned.1.call-start = ((), (), s32[]{:S(2)}) async-start(), calls=%async_computation.15 | async-start | bytes 8650752 | tf_op jit(solution)/shard_map/all_gather | solution.py:356
  89.7 422.9 %all-gather.26.cloned.1.call-start = ((), (), s32[]{:S(2)}) async-start(), calls=%async_computation.16 | async-start | bytes 4325376 | tf_op jit(solution)/shard_map/all_gather | solution.py:357
  90.4 511.3 %reduce-scatter.13.cloned.1.call-start = ((), (), s32[]{:S(2)}) async-start(), calls=%async_computation.17 | async-start | bytes 1179648 | tf_op jit(solution)/shard_map/reduce_scatter | solution.py:483
  217.5 31.1 %copy-start.28 = (f32[128,2,4,64]{0,3,2,1:T(8,128)}, f32[128,2,4,64]{0,3,2,1:T(8,128)S(1)}, u32[]{:S(2)}) copy-start(f32[128,2,4,64]{0,3,2,1:T(8,128)S(1)} %get-tuple-element.438) | copy-start | bytes 786436
  217.6 31.1 %copy-start.96 = (f32[2,4,128]{2,1,0:T(4,128)}, f32[2,4,128]{2,1,0:T(4,128)S(1)}, u32[]{:S(2)}) copy-start(f32[2,4,128]{2,1,0:T(4,128)S(1)} %get-tuple-element.1408) | copy-start | bytes 12292
  217.6 31.1 %copy-start.29 = (bf16[128,2,4,64]{0,3,2,1:T(8,128)(2,1)}, bf16[128,2,4,64]{0,3,2,1:T(8,128)(2,1)S(1)}, u32[]{:S(2)}) copy-start(bf16[128,2,4,64]{0,3,2,1:T(8,128)(2,1)S(1)} %convert_element_type.202) | copy-start | bytes 393220
  221.4 44.2 %copy-start.58 = (f32[128,128]{1,0:T(8,128)}, f32[128,128]{1,0:T(8,128)S(1)}, u32[]{:S(2)}) copy-start(f32[128,128]{1,0:T(8,128)S(1)} %fusion.134) | copy-start | bytes 196612
  274.3 95.4 %copy-start.41 = (f32[1536]{0:T(1024)S(1)}, f32[1536]{0:T(1024)}, u32[]{:S(2)}) copy-start(f32[1536]{0:T(1024)} %param.47) | copy-start | bytes 18436
  313.0 56.7 %copy-start.110 = (f32[128]{0:T(128)}, f32[128]{0:T(128)S(1)}, u32[]{:S(2)}) copy-start(f32[128]{0:T(128)S(1)} %get-tuple-element.775) | copy-start | bytes 1540
  313.0 60.2 %copy-start.80 = (f32[128]{0:T(128)}, f32[128]{0:T(128)S(1)}, u32[]{:S(2)}) copy-start(f32[128]{0:T(128)S(1)} %fusion.156) | copy-start | bytes 1540
  369.7 79.3 %copy-start.35 = (f32[1024]{0:T(1024)S(1)}, f32[1024]{0:T(1024)}, u32[]{:S(2)}) copy-start(f32[1024]{0:T(1024)} %param.46) | copy-start | bytes 12292
  373.2 75.8 %copy-start.105 = (f32[128]{0:T(128)}, f32[128]{0:T(128)S(1)}, u32[]{:S(2)}) copy-start(f32[128]{0:T(128)S(1)} %get-tuple-element.824) | copy-start | bytes 1540
  373.2 148.2 %copy-start.68 = (f32[128]{0:T(128)}, f32[128]{0:T(128)S(1)}, u32[]{:S(2)}) copy-start(f32[128]{0:T(128)S(1)} %fusion.157) | copy-start | bytes 1540
  449.0 63.5 %copy-start.26 = (bf16[1,128,1024]{2,1,0:T(8,128)(2,1)S(1)}, bf16[1,128,1024]{2,1,0:T(8,128)(2,1)}, u32[]{:S(2)}) copy-start(bf16[1,128,1024]{2,1,0:T(8,128)(2,1)} %param.53) | copy-start | bytes 786436
  532.8 131.3 %all-gather.30.cloned.1.call-start = ((), (), s32[]{:S(2)}) async-start(), calls=%async_computation.27 | async-start | bytes 3538944 | tf_op jit(solution)/shard_map/all_gather | solution.py:61
  543.9 282.8 %reduce-scatter.31.cloned.1.call-start = ((), (), s32[]{:S(2)}) async-start(), calls=%async_computation.28 | async-start | bytes 540672
  546.1 57.3 %copy-start.34 = (f32[128,64]{0,1:T(8,128)S(1)}, f32[128,64]{0,1:T(8,128)}, u32[]{:S(2)}) copy-start(f32[128,64]{0,1:T(8,128)} %get-tuple-element.808) | copy-start | bytes 98308
  603.4 91.7 %copy-start.37 = (bf16[128,128]{0,1:T(8,128)(2,1)}, bf16[128,128]{0,1:T(8,128)(2,1)S(1)}, u32[]{:S(2)}) copy-start(bf16[128,128]{0,1:T(8,128)(2,1)S(1)} %slice.298) | copy-start | bytes 98308
  604.3 90.8 %copy-start.39 = (bf16[128,128]{0,1:T(8,128)(2,1)}, bf16[128,128]{0,1:T(8,128)(2,1)S(1)}, u32[]{:S(2)}) copy-start(bf16[128,128]{0,1:T(8,128)(2,1)S(1)} %fusion.123) | copy-start | bytes 98308
  695.0 265.0 %reduce-scatter.17.cloned.1.call-start = ((), (), s32[]{:S(2)}) async-start(), calls=%async_computation.19 | async-start | bytes 1081344 | tf_op jit(solution)/shard_map/reduce_scatter | solution.py:547
  696.5 399.0 %reduce-scatter.15.cloned.1.call-start = ((), (), s32[]{:S(2)}) async-start(), calls=%async_computation.18 | async-start | bytes 2162688 | tf_op jit(solution)/shard_map/reduce_scatter | solution.py:544
  701.3 529.5 %reduce-scatter.19.cloned.1.call-start = ((), (), s32[]{:S(2)}) async-start(), calls=%async_computation.20 | async-start | bytes 2162688 | tf_op jit(solution)/shard_map/reduce_scatter | solution.py:464
  704.4 643.9 %reduce-scatter.25.cloned.1.call-start = ((), (), s32[]{:S(2)}) async-start(), calls=%async_computation.23 | async-start | bytes 6488064 | tf_op jit(solution)/shard_map/reduce_scatter | solution.py:465
  709.3 758.7 %reduce-scatter.21.cloned.1.call-start = ((), (), s32[]{:S(2)}) async-start(), calls=%async_computation.21 | async-start | bytes 6488064 | tf_op jit(solution)/shard_map/reduce_scatter | solution.py:550
  714.1 905.0 %reduce-scatter.29.cloned.1.call-start = ((), (), s32[]{:S(2)}) async-start(), calls=%async_computation.25 | async-start | bytes 8650752 | tf_op jit(solution)/shard_map/reduce_scatter | solution.py:467
  719.9 1044.8 %reduce-scatter.23.cloned.1.call-start = ((), (), s32[]{:S(2)}) async-start(), calls=%async_computation.22 | async-start | bytes 7569408 | tf_op jit(solution)/shard_map/reduce_scatter | solution.py:553
  740.2 5.8 collective-permute-start.1
  750.3 1196.2 %reduce-scatter.27.cloned.1.call-start = ((), (), s32[]{:S(2)}) async-start(), calls=%async_computation.24 | async-start | bytes 17301504 | tf_op jit(solution)/shard_map/reduce_scatter | solution.py:466
  771.2 40.1 %copy-start.102 = (f32[128]{0:T(128)S(1)}, f32[128]{0:T(128)}, u32[]{:S(2)}) copy-start(f32[128]{0:T(128)} %copy-done.101) | copy-start | bytes 1540
  771.2 40.1 %copy-start.13 = (f32[128,1024]{1,0:T(8,128)S(1)}, f32[128,1024]{1,0:T(8,128)}, u32[]{:S(2)}) copy-start(f32[128,1024]{1,0:T(8,128)} %copy-done.12) | copy-start | bytes 1572868
  771.2 40.1 %copy-start.27 = (bf16[1,128,1024]{2,1,0:T(8,128)(2,1)S(1)}, bf16[1,128,1024]{2,1,0:T(8,128)(2,1)}, u32[]{:S(2)}) copy-start(bf16[1,128,1024]{2,1,0:T(8,128)(2,1)} %param.53) | copy-start | bytes 786436
  771.2 40.1 %copy-start.70 = (f32[128]{0:T(128)S(1)}, f32[128]{0:T(128)}, u32[]{:S(2)}) copy-start(f32[128]{0:T(128)} %copy-done.68) | copy-start | bytes 1540
  771.3 40.1 %copy-start.98 = (f32[128]{0:T(128)S(1)}, f32[128]{0:T(128)}, u32[]{:S(2)}) copy-start(f32[128]{0:T(128)} %copy-done.97) | copy-start | bytes 1540
  (85 other events, 443.9 us)
Sparse Core Ops, SparseCore 0:
  10.9 63.2 all-gather.17
  77.0 52.8 all-gather.13
  132.8 52.7 all-gather.15
  188.1 60.4 all-gather.27
  251.4 57.6 all-gather.19
  311.8 57.8 all-gather.21
  372.6 76.3 all-gather.23
  451.9 60.6 all-gather.25
  532.9 68.7 reduce-scatter.12
  604.6 59.4 all-gather.29
  695.2 131.4 reduce-scatter.30
  829.3 130.7 reduce-scatter.16
  963.0 132.5 reduce-scatter.14
  1098.2 132.4 reduce-scatter.18
  1237.7 110.4 reduce-scatter.24
  1354.4 113.6 reduce-scatter.20
  1470.8 148.1 reduce-scatter.28
  1621.9 142.7 reduce-scatter.22
  1767.6 178.8 reduce-scatter.26
where the time goes:
time: 1960 us; the launch traced here: 1950 us
  waiting for transfers between devices  1520 us (78%)
  blocking collectives  173 us (9%)
  matrix products  117 us (6%)
  other arithmetic  61.4 us (3%)
  local copies, waits for them, and re-layouts  43.8 us (2%)
  between operations  19.9 us (1%)
    reduce_scatter x1, waiting for transfers between devices, per_device(): lax.psum_scatter(grad_gate_up_full, ('ctx', 'fsdp'), scatter_dimension=0,...  182 us
    reduce_scatter x1, waiting for transfers between devices, per_device(): lax.psum_scatter(grad_down_full, ('ctx', 'fsdp'), scatter_dimension=1, ti...  151 us
    reduce_scatter x1, waiting for transfers between devices, per_device(): lax.psum_scatter(product_left(normed_b, grad_conv_b), ('ctx', 'fsdp'), sc...  146 us
    reduce_scatter x1, waiting for transfers between devices, per_device(): lax.psum_scatter(product_left(normed_b, grad_query_b), ('ctx', 'fsdp'), s...  135 us
    reduce_scatter x1, waiting for transfers between devices, per_device(): lax.psum_scatter(grad_attn_out_full, ('ctx', 'fsdp'), scatter_dimension=1...  135 us
    reduce_scatter x1, waiting for transfers between devices, per_device(): lax.psum_scatter(product_left(normed_b, grad_keyval_b), ('ctx', 'fsdp'),...  132 us
    reduce_scatter x1, waiting for transfers between devices, per_device(): lax.psum_scatter(product_left(normed_b, grad_gate_b), ('ctx', 'fsdp'), sc...  120 us
    reduce_scatter x1, waiting for transfers between devices, per_device(): lax.psum_scatter(grad_mix_out_full, ('ctx', 'fsdp'), scatter_dimension=1,...  118 us
  transfers between devices with their start and end apart: 21, of which 19 were waited for; matrix products, arithmetic and copies ran while one was open for 9% of the time, Pallas kernels for 0%

commit v1 on v0

--- a/solution.py
+++ b/solution.py
@@ -30,52 +30,61 @@
     return lax.ppermute(block, axis, route)
 
 
-def entering(value, axis, combine, identity):
+def entering(decay, state, axis, sign):
+    count = lax.axis_size(axis)
+    heads, rows, width = state.shape
+
+    def hop(decay, state, distance):
+        packed = jnp.concatenate(
+            [
+                state.reshape(heads * rows, width),
+                jnp.broadcast_to(decay[:, None], (heads, width)),
+            ]
+        ).astype(jnp.bfloat16)
+        packed = from_behind(packed, axis, sign * distance).astype(jnp.float32)
+        return (packed[heads * rows :, 0], packed[: heads * rows].reshape(state.shape))
+
+    decay, state = hop(decay, state, 1)
+    distance = 1
+    while distance < count - 1:
+        before_decay, before_state = hop(decay, state, distance)
+        state = decay[:, None, None] * before_state + state
+        decay = before_decay * decay
+        distance *= 2
+    return state
+
+
+def swap_with(block, axis, distance):
+    route = [(i, i ^ distance) for i in range(lax.axis_size(axis))]
+    return lax.ppermute(block, axis, route)
+
+
+def gather_rows(block, axis):
     count, index = (lax.axis_size(axis), lax.axis_index(axis))
-    everything = jax.tree.map(
-        lambda part, kind: lax.all_gather(part.astype(kind), axis),
-        value,
-        (jnp.bfloat16, jnp.bfloat16),
-    )
-    start = jax.tree.map(
-        lambda part, zero: jnp.broadcast_to(jnp.asarray(zero, part.dtype), part.shape),
-        value,
-        identity,
-    )
-
-    def hop(k, before):
-        reached = k < index
-        new = combine(
-            before, jax.tree.map(lambda part, own: part[k].astype(own.dtype), everything, value)
-        )
-        return jax.tree.map(lambda a, b: jnp.where(reached, a, b), new, before)
-
-    return lax.fori_loop(0, count, hop, start)
-
-
-def entering_2(value, axis, join, neutral):
-    count = lax.axis_size(axis)
-    place = lax.axis_index(axis)
-    ahead = count - 1 - place
-    gathered = jax.tree.map(
-        lambda a, kind: lax.all_gather(a.astype(kind), axis),
-        value,
-        jax.tree.map(lambda a: jnp.bfloat16 if a.dtype == jnp.float32 else a.dtype, value),
-    )
-    state = jax.tree.map(lambda a, e: jnp.zeros_like(a) + jnp.asarray(e, a.dtype), value, neutral)
-
-    def one(hop, state):
-        source = count - 1 - hop
-        return join(
-            state,
-            jax.tree.map(
-                lambda a, own: lax.dynamic_index_in_dim(a, source, 0, False).astype(own.dtype),
-                gathered,
-                value,
-            ),
-        )
-
-    return lax.fori_loop(0, ahead, one, state)
+    rows, width = block.shape
+    distance, level = (count // 2, 0)
+    while distance:
+        other = swap_with(block, axis, distance)
+        upper = (index & distance) != 0
+        block = jnp.stack(
+            [jnp.where(upper, other, block), jnp.where(upper, block, other)], axis=level
+        )
+        distance, level = (distance // 2, level + 1)
+    return block.reshape(count * rows, width)
+
+
+def scatter_rows(values, axis):
+    count, index = (lax.axis_size(axis), lax.axis_index(axis))
+    rows, width = (values.shape[0] // count, values.shape[1])
+    distance, left = (1, count // 2)
+    while left:
+        pairs = values.reshape(left, 2, rows, width)
+        upper = (index & distance) != 0
+        kept = jnp.where(upper, pairs[:, 1], pairs[:, 0])
+        sent = jnp.where(upper, pairs[:, 0], pairs[:, 1]).astype(jnp.bfloat16)
+        values = kept + swap_with(sent, axis, distance).astype(jnp.float32)
+        distance, left = (distance * 2, left // 2)
+    return values.reshape(rows, width)
 
 
 def rms_scale(values, gain):
@@ -292,10 +301,6 @@
     y_total = y_local + coef_in[:, :, None] * carried + skip_gain[None, :, None] * mix_input
     gated = y_total.reshape(count_rows, DI) * jax.nn.silu(gate_values)
     return rms_scale(gated, gain_mix)
-
-
-def chain(earlier, later):
-    return (earlier[0] * later[0], later[0][:, None, None] * earlier[1] + later[1])
 
 
 def gate_product(gate_up):
@@ -333,40 +338,47 @@
     seg_ext = lax.dynamic_slice_in_dim(seg_pad, row_start, count_rows + KC - 1, 0)
     seg_before = seg_ext[KC - 2]
     positions = row_start + jnp.arange(count_rows, dtype=jnp.int32)
-    leading_block = jnp.searchsorted(seg_row, seg_own[0]) // block_length
+    leading_block = jnp.sum((seg_row < seg_own[0]).astype(jnp.int32)) // block_length
     required_flag = positions[-1] // block_length + 1
-    (
-        query_full,
-        keyval_full,
-        attn_out_full,
-        zgate_full,
-        conv_in_full,
-        step_full,
-        mix_out_full,
-        gate_up_full,
-        down_full,
-    ) = (
-        lax.all_gather(w_query, ("ctx", "fsdp"), axis=0, tiled=True),
-        lax.all_gather(key_value_weight, ("ctx", "fsdp"), axis=0, tiled=True),
-        lax.all_gather(w_attn_out, ("ctx", "fsdp"), axis=1, tiled=True),
-        lax.all_gather(w_zgate, ("ctx", "fsdp"), axis=0, tiled=True),
-        lax.all_gather(w_conv_in, ("ctx", "fsdp"), axis=0, tiled=True),
-        lax.all_gather(w_step, ("ctx", "fsdp"), axis=0, tiled=True),
-        lax.all_gather(w_mix_out, ("ctx", "fsdp"), axis=1, tiled=True),
-        lax.all_gather(w_gate_up, ("ctx", "fsdp"), axis=0, tiled=True),
-        lax.all_gather(w_down, ("ctx", "fsdp"), axis=1, tiled=True),
-    )
+    every = ("ctx", "fsdp")
+    in_widths = [
+        part.shape[1] for part in (w_query, key_value_weight, w_zgate, w_conv_in, w_step)
+    ]
+    in_cuts = [sum(in_widths[:k]) for k in range(1, 6)]
+    padding = -in_cuts[-1] % 128
+    w_in = lax.all_gather(
+        jnp.pad(
+            jnp.concatenate([w_query, key_value_weight, w_zgate, w_conv_in, w_step], axis=1),
+            ((0, 0), (0, padding)),
+        ),
+        every,
+        axis=0,
+        tiled=True,
+    )
+    w_rest = lax.all_gather(
+        jnp.concatenate([w_attn_out.T, w_mix_out.T, w_gate_up, w_down.T], axis=1),
+        every,
+        axis=0,
+        tiled=True,
+    )
+    attn_width = QUERY_HEADS * HEAD_SIZE
+    out_full = w_rest[:, : attn_width + DI]
+    gate_up_full = w_rest[:, attn_width + DI : attn_width + DI + 2 * FF]
+    down_full = w_rest[:, attn_width + DI + 2 * FF :]
     x_rows = tokens[0].astype(jnp.float32)
     normed, pull_in = jax.vjp(rms_scale, x_rows, gain_in)
     normed_b = normed.astype(jnp.bfloat16)
+    from_normed = product(normed_b, w_in)
+    query_raw, key_value_pair, gate_values, conv_raw, step_raw = jnp.split(
+        from_normed[:, : in_cuts[-1]], in_cuts[:-1], axis=1
+    )
     cosine_table, sine_table = angles(positions, HEAD_SIZE)
     query_rot = apply_rotation(
-        product(normed_b, query_full).reshape(count_rows, QUERY_HEADS, HEAD_SIZE),
+        query_raw.reshape(count_rows, QUERY_HEADS, HEAD_SIZE),
         cosine_table[:, None],
         sine_table[:, None],
     )
     query_batch = query_rot.astype(jnp.bfloat16)
-    key_value_pair = product(normed_b, keyval_full)
     key_rotated = apply_rotation(
         key_value_pair[:, : KEY_VALUE_HEADS * HEAD_SIZE].reshape(
             count_rows, KEY_VALUE_HEADS, HEAD_SIZE
@@ -381,15 +393,12 @@
         ],
         axis=1,
     ).astype(jnp.bfloat16)
-    all_kv = lax.all_gather(keyval_b, "ctx", axis=0, tiled=True)
+    all_kv = gather_rows(keyval_b, "ctx")
     attention_result, log_total = attend_forward(
         query_batch, all_kv, seg_row, seg_own, positions, leading_block, required_flag
     )
     attended_b = attention_result.astype(jnp.bfloat16)
-    attn_out = product(attended_b, attn_out_full)
-    gate_values = product(normed_b, zgate_full)
-    conv_in_b = product(normed_b, conv_in_full).astype(jnp.bfloat16)
-    step_raw = product(normed_b, step_full)
+    conv_in_b = conv_raw.astype(jnp.bfloat16)
     before_rows = from_behind(conv_in_b[count_rows - (KC - 1) :], "ctx", 1)
     extended = jnp.concatenate([before_rows, conv_in_b], axis=0).astype(jnp.float32)
     (activated, step_size, log_decay), pull_pre = jax.vjp(
@@ -407,8 +416,7 @@
         step_size,
         log_decay,
     )
-    identity = (jnp.ones_like(end_decay), jnp.zeros_like(state_local))
-    state_in = entering((end_decay, state_local), "ctx", chain, identity)[1]
+    state_in = entering(end_decay, state_local, "ctx", 1)
     mixed, pull_mix = jax.vjp(
         partial(mix_output, seg_own=seg_own, seg_before=seg_before),
         activated,
@@ -420,54 +428,41 @@
         state_in,
     )
     mixed_b = mixed.astype(jnp.bfloat16)
-    mix_out = product(mixed_b, mix_out_full)
-    hidden = x_rows + attn_out + mix_out
+    branches_b = jnp.concatenate([attended_b, mixed_b], axis=1)
+    hidden = x_rows + product_right(branches_b, out_full)
     hnorm, pull_ffn = jax.vjp(rms_scale, hidden, gain_ffn)
     hnorm_b = hnorm.astype(jnp.bfloat16)
     gate_up = product(hnorm_b, gate_up_full)
     ffn_act, pull_act = jax.vjp(gate_product, gate_up)
     ffn_act_b = ffn_act.astype(jnp.bfloat16)
-    result = hidden + product(ffn_act_b, down_full)
-    (
-        query_full,
-        keyval_full,
-        attn_out_full,
-        zgate_full,
-        conv_in_full,
-        step_full,
-        mix_out_full,
-        gate_up_full,
-        down_full,
-    ) = (
-        lax.all_gather(w_query, ("ctx", "fsdp"), axis=0, tiled=True),
-        lax.all_gather(key_value_weight, ("ctx", "fsdp"), axis=0, tiled=True),
-        lax.all_gather(w_attn_out, ("ctx", "fsdp"), axis=1, tiled=True),
-        lax.all_gather(w_zgate, ("ctx", "fsdp"), axis=0, tiled=True),
-        lax.all_gather(w_conv_in, ("ctx", "fsdp"), axis=0, tiled=True),
-        lax.all_gather(w_step, ("ctx", "fsdp"), axis=0, tiled=True),
-        lax.all_gather(w_mix_out, ("ctx", "fsdp"), axis=1, tiled=True),
-        lax.all_gather(w_gate_up, ("ctx", "fsdp"), axis=0, tiled=True),
-        lax.all_gather(w_down, ("ctx", "fsdp"), axis=1, tiled=True),
-    )
+    result = hidden + product_right(ffn_act_b, down_full)
     grad_result = cotangent[0].astype(jnp.float32)
     grad_result_b = grad_result.astype(jnp.bfloat16)
-    grad_down_full = product_left(ffn_act_b, grad_result_b)
-    (grad_gate_up_rows,) = pull_act(product_right(grad_result_b, down_full))
+    (grad_gate_up_rows,) = pull_act(product(grad_result_b, down_full))
     grad_gate_up_b = grad_gate_up_rows.astype(jnp.bfloat16)
-    grad_gate_up_full = product_left(hnorm_b, grad_gate_up_b)
     grad_hidden_norm, grad_gain_ffn = pull_ffn(product_right(grad_gate_up_b, gate_up_full))
     grad_hidden = grad_result + grad_hidden_norm
     grad_hidden_b = grad_hidden.astype(jnp.bfloat16)
-    grad_attn_out_full = product_left(attended_b, grad_hidden_b)
-    grad_mix_out_full = product_left(mixed_b, grad_hidden_b)
-    grad_attn_out, grad_mix_out, grad_gate_up, grad_down = (
-        lax.psum_scatter(grad_attn_out_full, ("ctx", "fsdp"), scatter_dimension=1, tiled=True),
-        lax.psum_scatter(grad_mix_out_full, ("ctx", "fsdp"), scatter_dimension=1, tiled=True),
-        lax.psum_scatter(grad_gate_up_full, ("ctx", "fsdp"), scatter_dimension=0, tiled=True),
-        lax.psum_scatter(grad_down_full, ("ctx", "fsdp"), scatter_dimension=1, tiled=True),
-    )
-    grad_attended_b = product_right(grad_hidden_b, attn_out_full).astype(jnp.bfloat16)
-    grad_mixed = product_right(grad_hidden_b, mix_out_full)
+    grad_rest = lax.psum_scatter(
+        jnp.concatenate(
+            [
+                product_left(grad_hidden_b, branches_b).astype(jnp.bfloat16),
+                product_left(hnorm_b, grad_gate_up_b).astype(jnp.bfloat16),
+                product_left(grad_result_b, ffn_act_b).astype(jnp.bfloat16),
+            ],
+            axis=1,
+        ),
+        every,
+        scatter_dimension=0,
+        tiled=True,
+    ).astype(jnp.float32)
+    grad_attn_out = grad_rest[:, :attn_width].T
+    grad_mix_out = grad_rest[:, attn_width : attn_width + DI].T
+    grad_gate_up = grad_rest[:, attn_width + DI : attn_width + DI + 2 * FF]
+    grad_down = grad_rest[:, attn_width + DI + 2 * FF :].T
+    grad_branches = product(grad_hidden_b, out_full)
+    grad_attended_b = grad_branches[:, :attn_width].astype(jnp.bfloat16)
+    grad_mixed = grad_branches[:, attn_width:]
     grad_query_rot, grad_kv_all = attend_backward(
         query_batch,
         all_kv,
@@ -480,7 +475,7 @@
         leading_block,
         required_flag,
     )
-    gradient_key_value_rows = lax.psum_scatter(grad_kv_all, "ctx", scatter_dimension=0, tiled=True)
+    gradient_key_value_rows = scatter_rows(grad_kv_all, "ctx")
     grad_query_b = (
         apply_rotation(grad_query_rot, cosine_table[:, None], -sine_table[:, None])
         .reshape(count_rows, QUERY_HEADS * HEAD_SIZE)
@@ -509,7 +504,7 @@
         grad_gain_mix,
         grad_state_in,
     ) = pull_mix(grad_mixed)
-    later_grads = entering_2((end_decay, grad_state_in), "ctx", chain, identity)[1]
+    later_grads = entering(end_decay, grad_state_in, "ctx", -1)
     grad_end_decay = jnp.sum(later_grads * state_in, axis=(1, 2))
     grad_act_state, grad_step_state, grad_decay_state = pull_state((grad_end_decay, later_grads))
     (
@@ -531,32 +526,24 @@
     grad_conv_b = grad_conv_rows.astype(jnp.bfloat16)
     grad_gate_b = grad_gate_values.astype(jnp.bfloat16)
     grad_step_b = grad_step_raw.astype(jnp.bfloat16)
-    grad_normed = (
-        product_right(grad_query_b, query_full)
-        + product_right(grad_keyval_b, keyval_full)
-        + product_right(grad_gate_b, zgate_full)
-        + product_right(grad_conv_b, conv_in_full)
-        + product_right(grad_step_b, step_full)
-    )
+    grad_from_normed = jnp.pad(
+        jnp.concatenate(
+            [grad_query_b, grad_keyval_b, grad_gate_b, grad_conv_b, grad_step_b], axis=1
+        ),
+        ((0, 0), (0, padding)),
+    )
+    grad_in = lax.psum_scatter(
+        product_left(normed_b, grad_from_normed).astype(jnp.bfloat16),
+        every,
+        scatter_dimension=0,
+        tiled=True,
+    ).astype(jnp.float32)
+    grad_query, grad_keyval, grad_zgate, grad_conv_in, grad_step = jnp.split(
+        grad_in[:, : in_cuts[-1]], in_cuts[:-1], axis=1
+    )
+    grad_normed = product_right(grad_from_normed, w_in)
     grad_x_norm, grad_gain_in = pull_in(grad_normed)
     grad_tokens = grad_hidden + grad_x_norm
-    grad_query, grad_keyval, grad_zgate, grad_conv_in, grad_step = (
-        lax.psum_scatter(
-            product_left(normed_b, grad_query_b), ("ctx", "fsdp"), scatter_dimension=0, tiled=True
-        ),
-        lax.psum_scatter(
-            product_left(normed_b, grad_keyval_b), ("ctx", "fsdp"), scatter_dimension=0, tiled=True
-        ),
-        lax.psum_scatter(
-            product_left(normed_b, grad_gate_b), ("ctx", "fsdp"), scatter_dimension=0, tiled=True
-        ),
-        lax.psum_scatter(
-            product_left(normed_b, grad_conv_b), ("ctx", "fsdp"), scatter_dimension=0, tiled=True
-        ),
-        lax.psum_scatter(
-            product_left(normed_b, grad_step_b), ("ctx", "fsdp"), scatter_dimension=0, tiled=True
-        ),
-    )
     (
         sum_gain_in,
         sum_gain_ffn,

time: 1960 us -> 758 us (0.39)
  waiting for transfers between devices: 1520 us -> 377 us
  blocking collectives: 173 us -> 44.1 us
  starting transfers between devices: 5.85 us -> 63 us
  matrix products: 117 us -> 81.1 us
  local copies, waits for them, and re-layouts: 43.8 us -> 71.8 us
  other arithmetic: 61.4 us -> 85.4 us
    reduce_scatter x9 -> x2, waiting for transfers between devices: 1170 us -> 238 us  [the longest x1 177 us: per_device(): lax.psum_scatter(jnp.concatenate([product_left(grad_hidden_b, branches_b)...]
    all_gather x9 -> x2, waiting for transfers between devices: 324 us -> 78.6 us  [the longest x1 64.9 us: per_device(): lax.all_gather(jnp.pad(jnp.concatenate([w_query, key_value_weight, w_zgat...]
    all_gather x4 -> x0, blocking collectives: 134 us -> none  [the longest x1 44.2 us: per_device(): lax.all_gather(w_step, ('ctx', 'fsdp'), axis=0, tiled=True)]
    ppermute x2 -> x10, waiting for transfers between devices: 5.08 us -> 54.9 us  [from_behind(): return lax.ppermute(block, axis, route)]
    ppermute x0 -> x6, starting transfers between devices: none -> 35.4 us  [swap_with(): return lax.ppermute(block, axis, route)]
    dot_general x8 -> x4, matrix products: 35.2 us -> 12.1 us  [product_left(): lax.dot_general(left, right, (((0,), (0,)), ((), ())), preferred_element_...]
    ppermute x2 -> x10, starting transfers between devices: 4.87 us -> 27.3 us  [from_behind(): return lax.ppermute(block, axis, route)]
  transfers between devices with their start and end apart: 21 -> 20, of which waited for: 19 -> 12; matrix products, arithmetic and copies ran while one was open for 9% -> 19% of each run, Pallas kernels for 0% -> 0%
where the time goes in v1:
time: 758 us; the launch traced here: 745 us
  waiting for transfers between devices  377 us (50%)
  other arithmetic  85.4 us (11%)
  matrix products  81.1 us (11%)
  local copies, waits for them, and re-layouts  71.8 us (9%)
  starting transfers between devices  63 us (8%)
  blocking collectives  44.1 us (6%)
  between operations  22.8 us (3%)
    reduce_scatter x1, waiting for transfers between devices, per_device(): lax.psum_scatter(jnp.concatenate([product_left(grad_hidden_b, branches_b)...  177 us
    all_gather x1, waiting for transfers between devices, per_device(): lax.all_gather(jnp.pad(jnp.concatenate([w_query, key_value_weight, w_zgat...  64.9 us
    reduce_scatter x1, waiting for transfers between devices, per_device(): lax.psum_scatter(product_left(normed_b, grad_from_normed).astype(jnp.bflo...  61.3 us
    ppermute x10, waiting for transfers between devices, from_behind(): return lax.ppermute(block, axis, route)  54.9 us
    psum x1, blocking collectives, per_device(): lax.psum((grad_gain_in, grad_gain_ffn, grad_gain_mix, grad_conv_weight, g...  44.1 us
    ppermute x6, starting transfers between devices, swap_with(): return lax.ppermute(block, axis, route)  35.4 us
    ppermute x10, starting transfers between devices, from_behind(): return lax.ppermute(block, axis, route)  27.3 us
    dot_general x4, matrix products, product_right(): lax.dot_general(left, right, (((1,), (1,)), ((), ())), preferred_element_...  19.1 us
  transfers between devices with their start and end apart: 20, of which 12 were waited for; matrix products, arithmetic and copies ran while one was open for 19% of the time, Pallas kernels for 0%

profile of v1, /device:TPU:0, one launch (start us, length us, event | category | flops | bytes accessed | tf_op | source)
XLA Modules:
  0.0 745.2 jit_solution(10250401069100493860)
XLA Ops:
  28.6 64.9 %all-gather.3.cloned.1.call-done = bf16[1024,4224]{1,0:T(8,128)(2,1)} async-done(((bf16[32,4224]{1,0:T(8,128)(2,1)}), bf16[1024,4224]{1,0:T(8,128)(2,1)}) %all-gather.3.cloned.1.call-update) | async-done | bytes 8650768 | tf_op jit(solution)/shard_map/all_gather | solution.py:349
  93.5 4.9 fusion.200
  99.4 3.3 collective-permute-start.3
  115.1 3.2 collective-permute-start.4
  124.6 2.3 copy.238
  128.6 8.0 %collective-permute-start.2 = (bf16[2,2,128,256]{3,2,0,1:T(8,128)(2,1)}, bf16[2,2,128,256]{3,2,0,1:T(8,128)(2,1)}, u32[]{:S(2)}, u32[]{:S(2)}) collective-permute-start(bf16[2,2,128,256]{3,2,0,1:T(8,128)(2,1)} %pad_maximum_fusion.15), channel_id=1, source_target_pairs={{0,4},{4,0},{8,12},{12,8},{16,20},{20,16},{24,28},{28,24},{1,5},{5... | collective-permute-start | bytes 786440 | tf_op jit(solution)/shard_map/ppermute | solution.py:59
  140.8 2.7 collective-permute-start.5
  146.4 2.7 collective-permute-done.2
  150.5 8.4 %collective-permute-done.5 = bf16[1560,128]{1,0:T(8,128)(2,1)} collective-permute-done((bf16[1560,128]{1,0:T(8,128)(2,1)}, bf16[1560,128]{1,0:T(8,128)(2,1)}, u32[]{:S(2)}, u32[]{:S(2)}) %collective-permute-start.5) | collective-permute-done | bytes 399392 | tf_op jit(solution)/shard_map/ppermute | solution.py:30
  163.3 4.5 collective-permute-start.6
  167.8 2.3 while.38
  170.9 4.4 collective-permute-done.6
  177.9 3.7 fusion.197
  182.7 6.9 collective-permute-start.7
  190.3 3.0 while.39
  190.6 2.6 fusion.257
  197.3 9.5 %collective-permute-done.7 = bf16[1560,128]{1,0:T(8,128)(2,1)} collective-permute-done((bf16[1560,128]{1,0:T(8,128)(2,1)}, bf16[1560,128]{1,0:T(8,128)(2,1)}, u32[]{:S(2)}, u32[]{:S(2)}) %collective-permute-start.7) | collective-permute-done | bytes 399392 | tf_op jit(solution)/shard_map/ppermute | solution.py:30
  210.6 3.3 fusion.62
  218.3 13.7 %all-gather.5.cloned.1.call-done = bf16[1024,8192]{1,0:T(8,128)(2,1)} async-done(((bf16[32,8192]{1,0:T(8,128)(2,1)}), bf16[1024,8192]{1,0:T(8,128)(2,1)}) %all-gather.5.cloned.1.call-update) | async-done | bytes 16777232 | tf_op jit(solution)/shard_map/all_gather | solution.py:358
  232.0 4.1 multiply_reduce_fusion.14
  236.1 5.6 fusion.30
  244.0 3.5 multiply_reduce_fusion.12
  250.1 3.1 multiply_reduce_fusion.6
  253.3 2.3 copy.239
  255.7 3.1 multiply_reduce_fusion.9
  258.8 3.1 fusion.56
  262.0 4.4 fusion.84
  268.3 7.2 while.40
  288.3 2.7 convolution_add_fusion
  293.5 2.3 copy.240
  302.4 12.6 %collective-permute-start.9 = (bf16[2,128,256]{2,1,0:T(8,128)(2,1)S(1)}, bf16[2,128,256]{2,1,0:T(8,128)(2,1)S(1)}, u32[]{:S(2)}, u32[]{:S(2)}) collective-permute-start(bf16[2,128,256]{2,1,0:T(8,128)(2,1)S(1)} %fusion.138), channel_id=1, source_target_pairs={{0,8},{4,12},{8,0},{12,4},{16,24},{20,28},{24,16},{28,20},{1,9},{5... | collective-permute-start | bytes 393224 | tf_op jit(solution)/shard_map/ppermute | solution.py:59
  318.7 11.1 %collective-permute-start.10 = (bf16[1,128,256]{2,1,0:T(8,128)(2,1)S(1)}, bf16[1,128,256]{2,1,0:T(8,128)(2,1)}, u32[]{:S(2)}, u32[]{:S(2)}) collective-permute-start(bf16[1,128,256]{2,1,0:T(8,128)(2,1)S(1)} %fusion.149), channel_id=1, source_target_pairs={{0,16},{4,20},{8,24},{12,28},{16,0},{20,4},{24,8},{28,12},{1,17},{... | collective-permute-start | bytes 196616 | tf_op jit(solution)/shard_map/ppermute | solution.py:59
  334.9 8.6 %collective-permute-done.12 = bf16[1560,128]{1,0:T(8,128)(2,1)S(1)} collective-permute-done((bf16[1560,128]{1,0:T(8,128)(2,1)}, bf16[1560,128]{1,0:T(8,128)(2,1)S(1)}, u32[]{:S(2)}, u32[]{:S(2)}) %collective-permute-start.12) | collective-permute-done | bytes 399392 | tf_op jit(solution)/shard_map/ppermute | solution.py:30
  346.9 8.6 %collective-permute-done.13 = bf16[1560,128]{1,0:T(8,128)(2,1)S(1)} collective-permute-done((bf16[1560,128]{1,0:T(8,128)(2,1)S(1)}, bf16[1560,128]{1,0:T(8,128)(2,1)S(1)}, u32[]{:S(2)}, u32[]{:S(2)}) %collective-permute-start.13) | collective-permute-done | bytes 399392 | tf_op jit(solution)/shard_map/ppermute | solution.py:30
  356.7 2.9 fusion.194
  362.0 2.5 fusion.129
  365.3 15.5 %collective-permute-done.14 = bf16[1560,128]{1,0:T(8,128)(2,1)} collective-permute-done((bf16[1560,128]{1,0:T(8,128)(2,1)}, bf16[1560,128]{1,0:T(8,128)(2,1)}, u32[]{:S(2)}, u32[]{:S(2)}) %collective-permute-start.14) | collective-permute-done | bytes 399392 | tf_op jit(solution)/shard_map/ppermute | solution.py:30
  383.0 3.1 multiply_reduce_fusion.5
  389.7 2.6 multiply_reduce_fusion.4
  399.0 2.7 multiply_reduce_fusion.8
  410.4 7.1 convolution_convert_fusion
  421.7 2.4 convolution_convert_fusion.1
  424.1 6.8 pad_maximum_fusion.1
  431.8 4.7 fusion.74
  436.7 6.8 fusion.117
  443.6 44.1 %all-reduce.20 = (f32[1024]{0:T(1024)}, f32[1024]{0:T(1024)}, f32[1536]{0:T(1024)}, f32[4,1792]{1,0:T(4,128)}, f32[1792]{0:T(1024)}, /*index=5*/f32[24]{0:T(128)}, f32[24]{0:T(128)}, f32[24]{0:T(128)}) all-reduce(f32[1024]{0:T(1024)S(1)} %get-tuple-element.518, ...), channel_id=1, replica_groups=mesh['ctx'=8,'fsdp'=4] {'ctx','fsdp'}, use_global_device_ids=true, to_apply=%region_28.29 | all-reduce | flops 12616 | bytes 100928 | tf_op jit(solution)/shard_map/psum | solution.py:556
  488.6 61.3 %reduce-scatter.3.cloned.1.call-done = bf16[32,4224]{1,0:T(8,128)(2,1)} async-done(((bf16[1024,4224]{1,0:T(8,128)(2,1)}), bf16[32,4224]{1,0:T(8,128)(2,1)}) %reduce-scatter.3.cloned.1.call-update) | async-done | bytes 270352 | tf_op jit(solution)/shard_map/reduce_scatter | solution.py:535
  557.2 177.2 %reduce-scatter.5.cloned.1.call-done = bf16[32,8192]{1,0:T(8,128)(2,1)} async-done(((bf16[1024,8192]{1,0:T(8,128)(2,1)}), bf16[32,8192]{1,0:T(8,128)(2,1)}) %reduce-scatter.5.cloned.1.call-update) | async-done | bytes 524304 | tf_op jit(solution)/shard_map/reduce_scatter | solution.py:446
  (580 shorter events, 158.2 us)
Async XLA Ops:
  7.2 86.3 %all-gather.3.cloned.1.call-start = ((), (), s32[]{:S(2)}) async-start(), calls=%async_computation.2 | async-start | bytes 8921088 | tf_op jit(solution)/shard_map/all_gather | solution.py:349
  8.8 17.5 %copy-start.103 = (f32[4,1792]{1,0:T(4,128)S(1)}, f32[4,1792]{1,0:T(4,128)}, u32[]{:S(2)}) copy-start(f32[4,1792]{1,0:T(4,128)} %param.42) | copy-start | bytes 86020
  9.5 16.8 %copy-start.6 = (bf16[1,128,1024]{2,1,0:T(8,128)(2,1)S(1)}, bf16[1,128,1024]{2,1,0:T(8,128)(2,1)}, u32[]{:S(2)}) copy-start(bf16[1,128,1024]{2,1,0:T(8,128)(2,1)} %param.28) | copy-start | bytes 786436
  10.5 16.1 %copy-start.154 = (f32[24]{0:T(128)S(1)}, f32[24]{0:T(128)}, u32[]{:S(2)}) copy-start(f32[24]{0:T(128)} %param.45) | copy-start | bytes 292
  11.4 82.1 %copy-start.62 = (f32[1024]{0:T(1024)S(1)}, f32[1024]{0:T(1024)}, u32[]{:S(2)}) copy-start(f32[1024]{0:T(1024)} %param.39) | copy-start | bytes 12292
  12.2 219.9 %all-gather.5.cloned.1.call-start = ((), (), s32[]{:S(2)}) async-start(), calls=%async_computation.3 | async-start | bytes 17301504 | tf_op jit(solution)/shard_map/all_gather | solution.py:358
  14.1 535.8 %reduce-scatter.3.cloned.1.call-start = ((), (), s32[]{:S(2)}) async-start(), calls=%async_computation.4 | async-start | bytes 8921088 | tf_op jit(solution)/shard_map/reduce_scatter | solution.py:535
  15.5 90.6 %copy-start.140 = (f32[128]{0:T(128)}, f32[128]{0:T(128)S(1)}, u32[]{:S(2)}) copy-start(f32[128]{0:T(128)S(1)} %get-tuple-element.603) | copy-start | bytes 1540
  25.3 73.1 %copy-start.57 = (f32[128,64]{0,1:T(8,128)}, f32[128,64]{0,1:T(8,128)S(1)}, u32[]{:S(2)}) copy-start(f32[128,64]{0,1:T(8,128)S(1)} %get-tuple-element.649) | copy-start | bytes 98308
  25.3 77.6 %copy-start.65 = (f32[128,64]{0,1:T(8,128)}, f32[128,64]{0,1:T(8,128)S(1)}, u32[]{:S(2)}) copy-start(f32[128,64]{0,1:T(8,128)S(1)} %get-tuple-element.648) | copy-start | bytes 98308
  26.3 82.5 %copy-start.80 = (f32[1792]{0:T(1024)}, f32[1792]{0:T(1024)S(1)}, u32[]{:S(2)}) copy-start(f32[1792]{0:T(1024)S(1)} %get-tuple-element.520) | copy-start | bytes 21508
  26.4 82.5 %copy-start.82 = (f32[1792]{0:T(1024)}, f32[1792]{0:T(1024)S(1)}, u32[]{:S(2)}) copy-start(f32[1792]{0:T(1024)S(1)} %get-tuple-element.521) | copy-start | bytes 21508
  26.4 82.5 %copy-start.84 = (f32[1792]{0:T(1024)}, f32[1792]{0:T(1024)S(1)}, u32[]{:S(2)}) copy-start(f32[1792]{0:T(1024)S(1)} %get-tuple-element.522) | copy-start | bytes 21508
  26.4 82.5 %copy-start.86 = (f32[1792]{0:T(1024)}, f32[1792]{0:T(1024)S(1)}, u32[]{:S(2)}) copy-start(f32[1792]{0:T(1024)S(1)} %get-tuple-element.523) | copy-start | bytes 21508
  26.5 67.0 %copy-start.147 = (f32[128]{0:T(128)}, f32[128]{0:T(128)S(1)}, u32[]{:S(2)}) copy-start(f32[128]{0:T(128)S(1)} %fusion.121) | copy-start | bytes 1540
  26.5 71.8 %copy-start.104 = (f32[128]{0:T(128)}, f32[128]{0:T(128)S(1)}, u32[]{:S(2)}) copy-start(f32[128]{0:T(128)S(1)} %fusion.176) | copy-start | bytes 1540
  26.6 79.3 %copy-start.144 = (f32[24]{0:T(128)}, f32[24]{0:T(128)S(1)}, u32[]{:S(2)}) copy-start(f32[24]{0:T(128)S(1)} %exponential_negate_fusion) | copy-start | bytes 292
  27.9 78.2 %copy-start.109 = (f32[128]{0:T(128)}, f32[128]{0:T(128)S(1)}, u32[]{:S(2)}) copy-start(f32[128]{0:T(128)S(1)} %get-tuple-element.656) | copy-start | bytes 1540
  99.4 9.3 %collective-permute-start.3 = (bf16[3,1792]{1,0:T(4,128)(2,1)}, bf16[3,1792]{1,0:T(4,128)(2,1)S(1)}, u32[]{:S(2)}, u32[]{:S(2)}) collective-permute-start(bf16[3,1792]{1,0:T(4,128)(2,1)} %slice.349), channel_id=1, source_target_pairs={{0,4},{4,8},{8,12},{12,16},{16,20},{20,24},{24,28},{1,5},{5,9},{9,... | collective-permute-start | bytes 32264 | tf_op jit(solution)/shard_map/ppermute | solution.py:30
  103.7 14.6 %collective-permute-start = (bf16[128,256]{1,0:T(8,128)(2,1)}, bf16[128,256]{1,0:T(8,128)(2,1)}, u32[]{:S(2)}, u32[]{:S(2)}) collective-permute-start(bf16[128,256]{1,0:T(8,128)(2,1)} %pad_maximum_fusion.17), channel_id=1, source_target_pairs={{0,16},{4,20},{8,24},{12,28},{16,0},{20,4},{24,8},{28,12},{1,17},{... | collective-permute-start | bytes 196616 | tf_op jit(solution)/shard_map/ppermute | solution.py:59
  105.9 15.4 %copy-start.35 = (f32[128,24]{1,0:T(8,128)}, f32[128,24]{1,0:T(8,128)S(1)}, u32[]{:S(2)}) copy-start(f32[128,24]{1,0:T(8,128)S(1)} %get-tuple-element.610) | copy-start | bytes 36868
  106.1 15.9 %copy-start.33 = (f32[128,24]{1,0:T(8,128)}, f32[128,24]{1,0:T(8,128)S(1)}, u32[]{:S(2)}) copy-start(f32[128,24]{1,0:T(8,128)S(1)} %reduce_window_sum.22) | copy-start | bytes 36868
  110.7 32.7 %copy-start.4 = (f32[128,1792]{1,0:T(8,128)}, f32[128,1792]{1,0:T(8,128)S(1)}, u32[]{:S(2)}) copy-start(f32[128,1792]{1,0:T(8,128)S(1)} %get-tuple-element.611) | copy-start | bytes 2752516
  113.3 148.7 %copy-start.1 = (f32[128,1536]{0,1:T(8,128)}, f32[128,1536]{0,1:T(8,128)S(1)}, u32[]{:S(2)}) copy-start(f32[128,1536]{0,1:T(8,128)S(1)} %copy.217) | copy-start | bytes 2359300
  115.1 21.5 %collective-permute-start.4 = (bf16[1560,128]{1,0:T(8,128)(2,1)}, bf16[1560,128]{1,0:T(8,128)(2,1)}, u32[]{:S(2)}, u32[]{:S(2)}) collective-permute-start(bf16[1560,128]{1,0:T(8,128)(2,1)} %pad_maximum_fusion.5), channel_id=1, source_target_pairs={{0,4},{4,8},{8,12},{12,16},{16,20},{20,24},{24,28},{1,5},{5,9},{9,... | collective-permute-start | bytes 1198088 | tf_op jit(solution)/shard_map/ppermute | solution.py:30
  120.6 6.3 collective-permute-start.1
  123.6 14.1 %copy-start.75 = (f32[128,24]{0,1:T(8,128)}, f32[128,24]{0,1:T(8,128)S(1)}, u32[]{:S(2)}) copy-start(f32[128,24]{0,1:T(8,128)S(1)} %copy.221) | copy-start | bytes 36868
  128.6 20.6 %collective-permute-start.2 = (bf16[2,2,128,256]{3,2,0,1:T(8,128)(2,1)}, bf16[2,2,128,256]{3,2,0,1:T(8,128)(2,1)}, u32[]{:S(2)}, u32[]{:S(2)}) collective-permute-start(bf16[2,2,128,256]{3,2,0,1:T(8,128)(2,1)} %pad_maximum_fusion.15), channel_id=1, source_target_pairs={{0,4},{4,0},{8,12},{12,8},{16,20},{20,16},{24,28},{28,24},{1,5},{5... | collective-permute-start | bytes 786440 | tf_op jit(solution)/shard_map/ppermute | solution.py:59
  140.8 18.1 %collective-permute-start.5 = (bf16[1560,128]{1,0:T(8,128)(2,1)}, bf16[1560,128]{1,0:T(8,128)(2,1)}, u32[]{:S(2)}, u32[]{:S(2)}) collective-permute-start(bf16[1560,128]{1,0:T(8,128)(2,1)} %pad_maximum_fusion.6), channel_id=1, source_target_pairs={{0,4},{4,8},{8,12},{12,16},{16,20},{20,24},{24,28},{1,5},{5,9},{9,... | collective-permute-start | bytes 1198088 | tf_op jit(solution)/shard_map/ppermute | solution.py:30
  163.3 12.0 %collective-permute-start.6 = (bf16[1560,128]{1,0:T(8,128)(2,1)}, bf16[1560,128]{1,0:T(8,128)(2,1)S(1)}, u32[]{:S(2)}, u32[]{:S(2)}) collective-permute-start(bf16[1560,128]{1,0:T(8,128)(2,1)} %pad_maximum_fusion.7), channel_id=1, source_target_pairs={{0,8},{4,12},{8,16},{12,20},{16,24},{20,28},{1,9},{5,13},{9,17},{1... | collective-permute-start | bytes 1198088 | tf_op jit(solution)/shard_map/ppermute | solution.py:30
  176.4 20.1 %copy-start.137 = (f32[24]{0:T(128)}, f32[24]{0:T(128)S(1)}, u32[]{:S(2)}) copy-start(f32[24]{0:T(128)S(1)} %get-tuple-element.605) | copy-start | bytes 292
  182.7 24.2 %collective-permute-start.7 = (bf16[1560,128]{1,0:T(8,128)(2,1)}, bf16[1560,128]{1,0:T(8,128)(2,1)}, u32[]{:S(2)}, u32[]{:S(2)}) collective-permute-start(bf16[1560,128]{1,0:T(8,128)(2,1)} %pad_maximum_fusion.8), channel_id=1, source_target_pairs={{0,16},{4,20},{8,24},{12,28},{1,17},{5,21},{9,25},{13,29},{2,18},{... | collective-permute-start | bytes 1198088 | tf_op jit(solution)/shard_map/ppermute | solution.py:30
  194.5 37.5 %copy-start.55 = (bf16[128,512]{1,0:T(8,128)(2,1)}, bf16[128,512]{1,0:T(8,128)(2,1)S(1)}, u32[]{:S(2)}) copy-start(bf16[128,512]{1,0:T(8,128)(2,1)S(1)} %copy.224) | copy-start | bytes 393220
  218.3 17.9 %copy-start.78 = (f32[1024]{0:T(1024)S(1)}, f32[1024]{0:T(1024)}, u32[]{:S(2)}) copy-start(f32[1024]{0:T(1024)} %param.40) | copy-start | bytes 12292
  275.5 12.7 %copy-start.88 = (f32[1536]{0:T(1024)S(1)}, f32[1536]{0:T(1024)}, u32[]{:S(2)}) copy-start(f32[1536]{0:T(1024)} %mul.943) | copy-start | bytes 18436
  281.1 20.1 %collective-permute-start.8 = (bf16[4,128,256]{2,1,0:T(8,128)(2,1)}, bf16[4,128,256]{2,1,0:T(8,128)(2,1)}, u32[]{:S(2)}, u32[]{:S(2)}) collective-permute-start(bf16[4,128,256]{2,1,0:T(8,128)(2,1)} %fusion.130), channel_id=1, source_target_pairs={{0,4},{4,0},{8,12},{12,8},{16,20},{20,16},{24,28},{28,24},{1,5},{5... | collective-permute-start | bytes 786440 | tf_op jit(solution)/shard_map/ppermute | solution.py:59
  285.9 43.9 %collective-permute-start.11 = (bf16[1560,128]{1,0:T(8,128)(2,1)}, bf16[1560,128]{1,0:T(8,128)(2,1)S(1)}, u32[]{:S(2)}, u32[]{:S(2)}) collective-permute-start(bf16[1560,128]{1,0:T(8,128)(2,1)} %pad_maximum_fusion.9), channel_id=1, source_target_pairs={{4,0},{8,4},{12,8},{16,12},{20,16},{24,20},{28,24},{5,1},{9,5},{13... | collective-permute-start | bytes 1198088 | tf_op jit(solution)/shard_map/ppermute | solution.py:30
  302.4 16.2 %collective-permute-start.9 = (bf16[2,128,256]{2,1,0:T(8,128)(2,1)S(1)}, bf16[2,128,256]{2,1,0:T(8,128)(2,1)S(1)}, u32[]{:S(2)}, u32[]{:S(2)}) collective-permute-start(bf16[2,128,256]{2,1,0:T(8,128)(2,1)S(1)} %fusion.138), channel_id=1, source_target_pairs={{0,8},{4,12},{8,0},{12,4},{16,24},{20,28},{24,16},{28,20},{1,9},{5... | collective-permute-start | bytes 393224 | tf_op jit(solution)/shard_map/ppermute | solution.py:59
  318.7 14.9 %collective-permute-start.10 = (bf16[1,128,256]{2,1,0:T(8,128)(2,1)S(1)}, bf16[1,128,256]{2,1,0:T(8,128)(2,1)}, u32[]{:S(2)}, u32[]{:S(2)}) collective-permute-start(bf16[1,128,256]{2,1,0:T(8,128)(2,1)S(1)} %fusion.149), channel_id=1, source_target_pairs={{0,16},{4,20},{8,24},{12,28},{16,0},{20,4},{24,8},{28,12},{1,17},{... | collective-permute-start | bytes 196616 | tf_op jit(solution)/shard_map/ppermute | solution.py:59
  330.0 25.9 %copy-start.132 = (f32[24]{0:T(128)}, f32[24]{0:T(128)S(1)}, u32[]{:S(2)}) copy-start(f32[24]{0:T(128)S(1)} %slice_reduce_fusion.2) | copy-start | bytes 292
  331.1 12.4 %collective-permute-start.12 = (bf16[1560,128]{1,0:T(8,128)(2,1)}, bf16[1560,128]{1,0:T(8,128)(2,1)S(1)}, u32[]{:S(2)}, u32[]{:S(2)}) collective-permute-start(bf16[1560,128]{1,0:T(8,128)(2,1)} %pad_maximum_fusion.10), channel_id=1, source_target_pairs={{4,0},{8,4},{12,8},{16,12},{20,16},{24,20},{28,24},{5,1},{9,5},{13... | collective-permute-start | bytes 1198088 | tf_op jit(solution)/shard_map/ppermute | solution.py:30
  344.3 11.3 %collective-permute-start.13 = (bf16[1560,128]{1,0:T(8,128)(2,1)S(1)}, bf16[1560,128]{1,0:T(8,128)(2,1)S(1)}, u32[]{:S(2)}, u32[]{:S(2)}) collective-permute-start(bf16[1560,128]{1,0:T(8,128)(2,1)S(1)} %pad_maximum_fusion.11), channel_id=1, source_target_pairs={{8,0},{12,4},{16,8},{20,12},{24,16},{28,20},{9,1},{13,5},{17,9},{2... | collective-permute-start | bytes 1198088 | tf_op jit(solution)/shard_map/ppermute | solution.py:30
  360.7 20.1 %collective-permute-start.14 = (bf16[1560,128]{1,0:T(8,128)(2,1)}, bf16[1560,128]{1,0:T(8,128)(2,1)}, u32[]{:S(2)}, u32[]{:S(2)}) collective-permute-start(bf16[1560,128]{1,0:T(8,128)(2,1)} %pad_maximum_fusion.12), channel_id=1, source_target_pairs={{16,0},{20,4},{24,8},{28,12},{17,1},{21,5},{25,9},{29,13},{18,2},{... | collective-permute-start | bytes 1198088 | tf_op jit(solution)/shard_map/ppermute | solution.py:30
  364.5 17.4 %copy-start.29 = (f32[1536,128]{1,0:T(8,128)S(1)}, f32[1536,128]{1,0:T(8,128)}, u32[]{:S(2)}) copy-start(f32[1536,128]{1,0:T(8,128)} %slice.385) | copy-start | bytes 2359300
  364.5 17.4 %copy-start.133 = (f32[24]{0:T(128)S(1)}, f32[24]{0:T(128)}, u32[]{:S(2)}) copy-start(f32[24]{0:T(128)} %copy-done.132) | copy-start | bytes 292
  394.8 13.0 %collective-permute-start.15 = (f32[3,1792]{1,0:T(4,128)}, f32[3,1792]{1,0:T(4,128)}, u32[]{:S(2)}, u32[]{:S(2)}) collective-permute-start(f32[3,1792]{1,0:T(4,128)} %pad_add_fusion.1), channel_id=1, source_target_pairs={{4,0},{8,4},{12,8},{16,12},{20,16},{24,20},{28,24},{5,1},{9,5},{13... | collective-permute-start | bytes 64520 | tf_op jit(solution)/shard_map/ppermute | solution.py:30
  417.5 316.9 %reduce-scatter.5.cloned.1.call-start = ((), (), s32[]{:S(2)}) async-start(), calls=%async_computation.5 | async-start | bytes 17301504 | tf_op jit(solution)/shard_map/reduce_scatter | solution.py:446
  436.7 50.9 %copy-start.148 = (f32[128]{0:T(128)S(1)}, f32[128]{0:T(128)}, u32[]{:S(2)}) copy-start(f32[128]{0:T(128)} %copy-done.147) | copy-start | bytes 1540
  (128 other events, 626.6 us)
Sparse Core Ops, SparseCore 0:
  12.3 81.1 all-gather.2
  96.9 135.0 all-gather.4
  417.6 132.2 reduce-scatter.2
  552.1 182.2 reduce-scatter.4

commit v2 on v1

--- a/solution.py
+++ b/solution.py
@@ -532,8 +532,9 @@
         ),
         ((0, 0), (0, padding)),
     )
+    after_rest = jnp.minimum(jnp.abs(grad_rest[0, 0]), 0.0)
     grad_in = lax.psum_scatter(
-        product_left(normed_b, grad_from_normed).astype(jnp.bfloat16),
+        (product_left(normed_b, grad_from_normed) + after_rest).astype(jnp.bfloat16),
         every,
         scatter_dimension=0,
         tiled=True,

time: 758 us -> 637 us (0.84)
  waiting for transfers between devices: 377 us -> 227 us
  local copies, waits for them, and re-layouts: 71.8 us -> 83.2 us
    reduce_scatter x1, waiting for transfers between devices: 177 us -> 11.9 us  [per_device(): lax.psum_scatter(jnp.concatenate([product_left(grad_hidden_b, branches_b)...]
    reduce_scatter x1, waiting for transfers between devices: 61.3 us -> 72.6 us  [per_device(): lax.psum_scatter((product_left(normed_b, grad_from_normed) + after_rest)....]
    unnamed x321 -> x305, local copies, waits for them, and re-layouts: 16.1 us -> 20.6 us
  transfers between devices with their start and end apart: 20 -> 20, of which waited for: 12 -> 13; matrix products, arithmetic and copies ran while one was open for 19% -> 31% of each run, Pallas kernels for 0% -> 0%
where the time goes in v2:
time: 637 us; the launch traced here: 625 us
  waiting for transfers between devices  227 us (36%)
  other arithmetic  86.6 us (14%)
  matrix products  85.7 us (13%)
  local copies, waits for them, and re-layouts  83.2 us (13%)
  starting transfers between devices  69.7 us (11%)
  blocking collectives  49.1 us (8%)
  between operations  23.6 us (4%)
    reduce_scatter x1, waiting for transfers between devices, per_device(): lax.psum_scatter((product_left(normed_b, grad_from_normed) + after_rest)....  72.6 us
    all_gather x1, waiting for transfers between devices, per_device(): lax.all_gather(jnp.pad(jnp.concatenate([w_query, key_value_weight, w_zgat...  64.8 us
    ppermute x10, waiting for transfers between devices, from_behind(): return lax.ppermute(block, axis, route)  56.7 us
    psum x1, blocking collectives, per_device(): lax.psum((grad_gain_in, grad_gain_ffn, grad_gain_mix, grad_conv_weight, g...  49.1 us
    ppermute x6, starting transfers between devices, swap_with(): return lax.ppermute(block, axis, route)  37.7 us
    ppermute x10, starting transfers between devices, from_behind(): return lax.ppermute(block, axis, route)  31.8 us
    dot_general x4, matrix products, product_right(): lax.dot_general(left, right, (((1,), (1,)), ((), ())), preferred_element_...  21.9 us
    unnamed x305, local copies, waits for them, and re-layouts  20.6 us
  transfers between devices with their start and end apart: 20, of which 13 were waited for; matrix products, arithmetic and copies ran while one was open for 31% of the time, Pallas kernels for 0%

profile of v2, /device:TPU:0, one launch (start us, length us, event | category | flops | bytes accessed | tf_op | source)
XLA Modules:
  0.0 625.1 jit_solution(16013402175801970528)
XLA Ops:
  28.8 64.8 %all-gather.3.cloned.1.call-done = bf16[1024,4224]{1,0:T(8,128)(2,1)} async-done(((bf16[32,4224]{1,0:T(8,128)(2,1)}), bf16[1024,4224]{1,0:T(8,128)(2,1)}) %all-gather.3.cloned.1.call-update) | async-done | bytes 8650768 | tf_op jit(solution)/shard_map/all_gather | solution.py:349
  93.6 4.9 fusion.200
  99.5 3.3 collective-permute-start.3
  109.0 2.5 fusion.87
  115.8 2.5 collective-permute-start.4
  127.6 9.8 %collective-permute-start.2 = (bf16[2,2,128,256]{3,2,0,1:T(8,128)(2,1)}, bf16[2,2,128,256]{3,2,0,1:T(8,128)(2,1)}, u32[]{:S(2)}, u32[]{:S(2)}) collective-permute-start(bf16[2,2,128,256]{3,2,0,1:T(8,128)(2,1)} %pad_maximum_fusion.15), channel_id=1, source_target_pairs={{0,4},{4,0},{8,12},{12,8},{16,20},{20,16},{24,28},{28,24},{1,5},{5... | collective-permute-start | bytes 786440 | tf_op jit(solution)/shard_map/ppermute | solution.py:59
  139.6 2.7 collective-permute-start.5
  144.2 5.7 collective-permute-done.2
  153.2 5.1 collective-permute-done.5
  162.7 8.1 %collective-permute-start.6 = (bf16[1560,128]{1,0:T(8,128)(2,1)}, bf16[1560,128]{1,0:T(8,128)(2,1)}, u32[]{:S(2)}, u32[]{:S(2)}) collective-permute-start(bf16[1560,128]{1,0:T(8,128)(2,1)} %pad_maximum_fusion.7), channel_id=1, source_target_pairs={{0,8},{4,12},{8,16},{12,20},{16,24},{20,28},{1,9},{5,13},{9,17},{1... | collective-permute-start | bytes 1198088 | tf_op jit(solution)/shard_map/ppermute | solution.py:30
  170.7 3.4 while.38
  181.3 3.0 fusion.197
  185.3 8.3 %collective-permute-start.7 = (bf16[1560,128]{1,0:T(8,128)(2,1)}, bf16[1560,128]{1,0:T(8,128)(2,1)}, u32[]{:S(2)}, u32[]{:S(2)}) collective-permute-start(bf16[1560,128]{1,0:T(8,128)(2,1)} %pad_maximum_fusion.8), channel_id=1, source_target_pairs={{0,16},{4,20},{8,24},{12,28},{1,17},{5,21},{9,25},{13,29},{2,18},{... | collective-permute-start | bytes 1198088 | tf_op jit(solution)/shard_map/ppermute | solution.py:30
  194.3 4.6 while.39
  196.0 2.7 fusion.257
  204.4 5.0 collective-permute-done.7
  211.5 4.1 fusion.62
  220.3 11.0 %all-gather.5.cloned.1.call-done = bf16[1024,8192]{1,0:T(8,128)(2,1)} async-done(((bf16[32,8192]{1,0:T(8,128)(2,1)}), bf16[1024,8192]{1,0:T(8,128)(2,1)}) %all-gather.5.cloned.1.call-update) | async-done | bytes 16777232 | tf_op jit(solution)/shard_map/all_gather | solution.py:358
  231.3 3.9 multiply_reduce_fusion.14
  235.2 4.9 fusion.30
  240.1 3.5 fusion.142
  243.7 2.4 convolution_convert_fusion
  246.1 7.0 %multiply_reduce_fusion.12 = (f32[1024]{0:T(1024)}, f32[128]{0:T(128)S(1)}, f32[128,1024]{1,0:T(8,128)S(1)}) fusion(f32[128,1024]{1,0:T(8,128)S(1)} %get-tuple-element.660, f32[128]{0:T(128)S(1)} %fusion.178, f32[1024]{0:T(1024)S(1)} %copy-done.84, bf16[1024,8192]{1,0:T(8,128)(2,1)} %all-gather.5.cloned.1.call-done, ...), kind=kOutput, calls=%fused_computation.182 | convolution fusion | flops 1075575680 | bytes 11543552 | tf_op jit(solution)/shard_map/dot_general | solution.py:118
  257.1 6.7 %pad_maximum_fusion.1 = bf16[1024,8192]{1,0:T(8,128)(2,1)} fusion(bf16[1024,2048]{1,0:T(8,128)(2,1)S(1)} %convert_bitcast_fusion, bf16[1024,4096]{1,0:T(8,128)(2,1)S(1)} %convolution_convert_fusion, bf16[1024,2048]{1,0:T(8,128)(2,1)S(1)} %convolution_convert_fusion.1), kind=kLoop, calls=%fused_computation.48 | loop fusion | flops 50331648 | bytes 33554432 | tf_op jit(solution)/shard_map/concatenate | solution.py:447
  269.4 3.0 fusion.36
  275.4 7.2 %while.40 = (s32[]{:T(128)}, f32[128,2,4,64]{0,3,2,1:T(8,128)}, f32[1024,256]{1,0:T(8,128)}, s32[]{:T(128)}, bf16[1024,256]{0,1:T(8,128)(2,1)S(1)}, /*index=5*/s...) while((s32[]{:T(128)}, f32[128,2,4,64]{0,3,2,1:T(8,128)}, ...), condition=%wide.region_13.14_spmd.clone, body=%wide.region_12.13_spmd.clone.sunk | while | flops 339739264 | bytes 15224567 | solution.py:248
  298.6 4.3 fusion.84
  305.2 2.7 fusion.56
  307.9 2.7 convolution_add_fusion
  315.0 2.3 copy.240
  325.6 12.4 %collective-permute-start.9 = (bf16[2,128,256]{2,1,0:T(8,128)(2,1)S(1)}, bf16[2,128,256]{2,1,0:T(8,128)(2,1)S(1)}, u32[]{:S(2)}, u32[]{:S(2)}) collective-permute-start(bf16[2,128,256]{2,1,0:T(8,128)(2,1)S(1)} %fusion.138), channel_id=1, source_target_pairs={{0,8},{4,12},{8,0},{12,4},{16,24},{20,28},{24,16},{28,20},{1,9},{5... | collective-permute-start | bytes 393224 | tf_op jit(solution)/shard_map/ppermute | solution.py:59
  339.7 2.7 collective-permute-done.9
  342.5 11.7 %collective-permute-start.10 = (bf16[1,128,256]{2,1,0:T(8,128)(2,1)S(1)}, bf16[1,128,256]{2,1,0:T(8,128)(2,1)}, u32[]{:S(2)}, u32[]{:S(2)}) collective-permute-start(bf16[1,128,256]{2,1,0:T(8,128)(2,1)S(1)} %fusion.149), channel_id=1, source_target_pairs={{0,16},{4,20},{8,24},{12,28},{16,0},{20,4},{24,8},{28,12},{1,17},{... | collective-permute-start | bytes 196616 | tf_op jit(solution)/shard_map/ppermute | solution.py:59
  362.1 11.2 %collective-permute-done.12 = bf16[1560,128]{1,0:T(8,128)(2,1)S(1)} collective-permute-done((bf16[1560,128]{1,0:T(8,128)(2,1)}, bf16[1560,128]{1,0:T(8,128)(2,1)S(1)}, u32[]{:S(2)}, u32[]{:S(2)}) %collective-permute-start.12) | collective-permute-done | bytes 399392 | tf_op jit(solution)/shard_map/ppermute | solution.py:30
  378.7 15.2 %collective-permute-done.13 = bf16[1560,128]{1,0:T(8,128)(2,1)S(1)} collective-permute-done((bf16[1560,128]{1,0:T(8,128)(2,1)S(1)}, bf16[1560,128]{1,0:T(8,128)(2,1)S(1)}, u32[]{:S(2)}, u32[]{:S(2)}) %collective-permute-start.13) | collective-permute-done | bytes 399392 | tf_op jit(solution)/shard_map/ppermute | solution.py:30
  396.4 3.2 fusion.194
  402.1 2.5 fusion.129
  405.8 20.1 %collective-permute-done.14 = bf16[1560,128]{1,0:T(8,128)(2,1)} collective-permute-done((bf16[1560,128]{1,0:T(8,128)(2,1)}, bf16[1560,128]{1,0:T(8,128)(2,1)}, u32[]{:S(2)}, u32[]{:S(2)}) %collective-permute-start.14) | collective-permute-done | bytes 399392 | tf_op jit(solution)/shard_map/ppermute | solution.py:30
  428.5 2.5 multiply_reduce_fusion.5
  431.0 2.4 copy.241
  434.9 2.6 multiply_reduce_fusion.4
  440.6 2.3 multiply_reduce_fusion.8
  452.1 11.9 %reduce-scatter.3.cloned.1.call-done = bf16[32,8192]{1,0:T(8,128)(2,1)} async-done(((bf16[1024,8192]{1,0:T(8,128)(2,1)}), bf16[32,8192]{1,0:T(8,128)(2,1)}) %reduce-scatter.3.cloned.1.call-update) | async-done | bytes 524304 | tf_op jit(solution)/shard_map/reduce_scatter | solution.py:446
  465.7 7.2 %add_convert_fusion = bf16[1024,4224]{1,0:T(8,128)(2,1)} fusion(f32[]{:T(128)} %bitcast.80, bf16[128,4120]{1,0:T(8,128)(2,1)} %convert_dynamic-update-slice_fusion.1, bf16[1,128,1024]{2,1,0:T(8,128)(2,1)S(1)} %copy-done.8, f32[1024]{0:T(1024)S(1)} %copy-done.63, f32[128]{0:T(128)S(1)} %copy-done.103), kind=kOutput, calls=%fused_computation.47 | convolution fusion | flops 1116471296 | bytes 9972228 | tf_op jit(solution)/shard_map/dot_general | solution.py:112
  474.1 4.5 fusion.74
  478.8 6.5 %fusion.117 = (f32[1024]{0:T(1024)S(1)}, f32[128]{0:T(128)S(1)}, f32[128,1024]{1,0:T(8,128)S(1)}) fusion(bf16[1,128,1024]{2,1,0:T(8,128)(2,1)S(1)} %copy-done.8, f32[128]{0:T(128)S(1)} %copy-done.103, f32[1024]{0:T(1024)S(1)} %copy-done.63, bf16[1024,4224]{1,0:T(8,128)(2,1)} %all-gather.3.cloned.1.call-done, bf16[128,4120]{1,0:T(8,128)(2,1)S(1)} %copy-done.23), kind=kOutput, calls=%fused_computation.172 | convolution fusion | flops 1108212608 | bytes 10501120 | tf_op jit(solution)/shard_map/dot_general | solution.py:118
  485.3 49.1 %all-reduce.20 = (f32[1024]{0:T(1024)}, f32[1024]{0:T(1024)}, f32[1536]{0:T(1024)}, f32[4,1792]{1,0:T(4,128)}, f32[1792]{0:T(1024)}, /*index=5*/f32[24]{0:T(128)}, f32[24]{0:T(128)}, f32[24]{0:T(128)}) all-reduce(f32[1024]{0:T(1024)S(1)} %get-tuple-element.518, ...), channel_id=1, replica_groups=mesh['ctx'=8,'fsdp'=4] {'ctx','fsdp'}, use_global_device_ids=true, to_apply=%region_28.29 | all-reduce | flops 12616 | bytes 100928 | tf_op jit(solution)/shard_map/psum | solution.py:557
  538.4 72.6 %reduce-scatter.5.cloned.1.call-done = bf16[32,4224]{1,0:T(8,128)(2,1)} async-done(((bf16[1024,4224]{1,0:T(8,128)(2,1)}), bf16[32,4224]{1,0:T(8,128)(2,1)}) %reduce-scatter.5.cloned.1.call-update) | async-done | bytes 270352 | tf_op jit(solution)/shard_map/reduce_scatter | solution.py:536
  (565 shorter events, 173.8 us)
Async XLA Ops:
  7.2 18.2 %copy-start.101 = (f32[4,1792]{1,0:T(4,128)S(1)}, f32[4,1792]{1,0:T(4,128)}, u32[]{:S(2)}) copy-start(f32[4,1792]{1,0:T(4,128)} %param.42) | copy-start | bytes 86020
  7.2 18.9 %copy-start.7 = (bf16[1,128,1024]{2,1,0:T(8,128)(2,1)S(1)}, bf16[1,128,1024]{2,1,0:T(8,128)(2,1)}, u32[]{:S(2)}) copy-start(bf16[1,128,1024]{2,1,0:T(8,128)(2,1)} %param.28) | copy-start | bytes 786436
  7.2 19.6 %copy-start.146 = (f32[24]{0:T(128)S(1)}, f32[24]{0:T(128)}, u32[]{:S(2)}) copy-start(f32[24]{0:T(128)} %param.45) | copy-start | bytes 292
  7.2 86.3 %copy-start.63 = (f32[1024]{0:T(1024)S(1)}, f32[1024]{0:T(1024)}, u32[]{:S(2)}) copy-start(f32[1024]{0:T(1024)} %param.39) | copy-start | bytes 12292
  7.2 86.3 %all-gather.3.cloned.1.call-start = ((), (), s32[]{:S(2)}) async-start(), calls=%async_computation.2 | async-start | bytes 8921088 | tf_op jit(solution)/shard_map/all_gather | solution.py:349
  12.2 219.1 %all-gather.5.cloned.1.call-start = ((), (), s32[]{:S(2)}) async-start(), calls=%async_computation.3 | async-start | bytes 17301504 | tf_op jit(solution)/shard_map/all_gather | solution.py:358
  14.1 449.8 %reduce-scatter.3.cloned.1.call-start = ((), (), s32[]{:S(2)}) async-start(), calls=%async_computation.4 | async-start | bytes 17301504 | tf_op jit(solution)/shard_map/reduce_scatter | solution.py:446
  15.5 90.7 %copy-start.131 = (f32[128]{0:T(128)}, f32[128]{0:T(128)S(1)}, u32[]{:S(2)}) copy-start(f32[128]{0:T(128)S(1)} %get-tuple-element.603) | copy-start | bytes 1540
  25.3 77.7 %copy-start.66 = (f32[128,64]{0,1:T(8,128)}, f32[128,64]{0,1:T(8,128)S(1)}, u32[]{:S(2)}) copy-start(f32[128,64]{0,1:T(8,128)S(1)} %get-tuple-element.648) | copy-start | bytes 98308
  25.4 77.7 %copy-start.52 = (f32[128,128]{1,0:T(8,128)}, f32[128,128]{1,0:T(8,128)S(1)}, u32[]{:S(2)}) copy-start(f32[128,128]{1,0:T(8,128)S(1)} %copy.209) | copy-start | bytes 196612
  26.1 82.8 %copy-start.85 = (f32[1792]{0:T(1024)}, f32[1792]{0:T(1024)S(1)}, u32[]{:S(2)}) copy-start(f32[1792]{0:T(1024)S(1)} %get-tuple-element.520) | copy-start | bytes 21508
  26.1 82.9 %copy-start.87 = (f32[1792]{0:T(1024)}, f32[1792]{0:T(1024)S(1)}, u32[]{:S(2)}) copy-start(f32[1792]{0:T(1024)S(1)} %get-tuple-element.521) | copy-start | bytes 21508
  26.1 82.9 %copy-start.89 = (f32[1792]{0:T(1024)}, f32[1792]{0:T(1024)S(1)}, u32[]{:S(2)}) copy-start(f32[1792]{0:T(1024)S(1)} %get-tuple-element.522) | copy-start | bytes 21508
  26.8 71.6 %copy-start.102 = (f32[128]{0:T(128)}, f32[128]{0:T(128)S(1)}, u32[]{:S(2)}) copy-start(f32[128]{0:T(128)S(1)} %fusion.176) | copy-start | bytes 1540
  26.8 79.0 %copy-start.136 = (f32[24]{0:T(128)}, f32[24]{0:T(128)S(1)}, u32[]{:S(2)}) copy-start(f32[24]{0:T(128)S(1)} %exponential_negate_fusion) | copy-start | bytes 292
  28.1 78.1 %copy-start.106 = (f32[128]{0:T(128)}, f32[128]{0:T(128)S(1)}, u32[]{:S(2)}) copy-start(f32[128]{0:T(128)S(1)} %get-tuple-element.656) | copy-start | bytes 1540
  28.1 80.9 %copy-start.112 = (pred[128]{0:T(512)(128)(4,1)}, pred[128]{0:T(512)(128)(4,1)S(1)}, u32[]{:S(2)}) copy-start(pred[128]{0:T(512)(128)(4,1)S(1)} %get-tuple-element.650) | copy-start | bytes 388
  99.5 9.3 %collective-permute-start.3 = (bf16[3,1792]{1,0:T(4,128)(2,1)S(1)}, bf16[3,1792]{1,0:T(4,128)(2,1)S(1)}, u32[]{:S(2)}, u32[]{:S(2)}) collective-permute-start(bf16[3,1792]{1,0:T(4,128)(2,1)S(1)} %slice.353), channel_id=1, source_target_pairs={{0,4},{4,8},{8,12},{12,16},{16,20},{20,24},{24,28},{1,5},{5,9},{9,... | collective-permute-start | bytes 32264 | tf_op jit(solution)/shard_map/ppermute | solution.py:30
  103.8 14.5 %collective-permute-start = (bf16[128,256]{1,0:T(8,128)(2,1)}, bf16[128,256]{1,0:T(8,128)(2,1)}, u32[]{:S(2)}, u32[]{:S(2)}) collective-permute-start(bf16[128,256]{1,0:T(8,128)(2,1)} %pad_maximum_fusion.17), channel_id=1, source_target_pairs={{0,16},{4,20},{8,24},{12,28},{16,0},{20,4},{24,8},{28,12},{1,17},{... | collective-permute-start | bytes 196616 | tf_op jit(solution)/shard_map/ppermute | solution.py:59
  111.4 99.0 %copy-start.5 = (f32[128,1792]{1,0:T(8,128)}, f32[128,1792]{1,0:T(8,128)S(1)}, u32[]{:S(2)}) copy-start(f32[128,1792]{1,0:T(8,128)S(1)} %get-tuple-element.611) | copy-start | bytes 2752516
  113.9 97.5 %copy-start.2 = (f32[128,1536]{0,1:T(8,128)}, f32[128,1536]{0,1:T(8,128)S(1)}, u32[]{:S(2)}) copy-start(f32[128,1536]{0,1:T(8,128)S(1)} %copy.217) | copy-start | bytes 2359300
  115.8 21.6 %collective-permute-start.4 = (bf16[1560,128]{1,0:T(8,128)(2,1)}, bf16[1560,128]{1,0:T(8,128)(2,1)S(1)}, u32[]{:S(2)}, u32[]{:S(2)}) collective-permute-start(bf16[1560,128]{1,0:T(8,128)(2,1)} %pad_maximum_fusion.5), channel_id=1, source_target_pairs={{0,4},{4,8},{8,12},{12,16},{16,20},{20,24},{24,28},{1,5},{5,9},{9,... | collective-permute-start | bytes 1198088 | tf_op jit(solution)/shard_map/ppermute | solution.py:30
  120.5 5.3 collective-permute-start.1
  127.6 22.4 %collective-permute-start.2 = (bf16[2,2,128,256]{3,2,0,1:T(8,128)(2,1)}, bf16[2,2,128,256]{3,2,0,1:T(8,128)(2,1)}, u32[]{:S(2)}, u32[]{:S(2)}) collective-permute-start(bf16[2,2,128,256]{3,2,0,1:T(8,128)(2,1)} %pad_maximum_fusion.15), channel_id=1, source_target_pairs={{0,4},{4,0},{8,12},{12,8},{16,20},{20,16},{24,28},{28,24},{1,5},{5... | collective-permute-start | bytes 786440 | tf_op jit(solution)/shard_map/ppermute | solution.py:59
  139.6 18.7 %collective-permute-start.5 = (bf16[1560,128]{1,0:T(8,128)(2,1)}, bf16[1560,128]{1,0:T(8,128)(2,1)}, u32[]{:S(2)}, u32[]{:S(2)}) collective-permute-start(bf16[1560,128]{1,0:T(8,128)(2,1)} %pad_maximum_fusion.6), channel_id=1, source_target_pairs={{0,4},{4,8},{8,12},{12,16},{16,20},{20,24},{24,28},{1,5},{5,9},{9,... | collective-permute-start | bytes 1198088 | tf_op jit(solution)/shard_map/ppermute | solution.py:30
  162.7 13.0 %collective-permute-start.6 = (bf16[1560,128]{1,0:T(8,128)(2,1)}, bf16[1560,128]{1,0:T(8,128)(2,1)}, u32[]{:S(2)}, u32[]{:S(2)}) collective-permute-start(bf16[1560,128]{1,0:T(8,128)(2,1)} %pad_maximum_fusion.7), channel_id=1, source_target_pairs={{0,8},{4,12},{8,16},{12,20},{16,24},{20,28},{1,9},{5,13},{9,17},{1... | collective-permute-start | bytes 1198088 | tf_op jit(solution)/shard_map/ppermute | solution.py:30
  178.4 32.0 %copy-start.123 = (f32[24]{0:T(128)}, f32[24]{0:T(128)S(1)}, u32[]{:S(2)}) copy-start(f32[24]{0:T(128)S(1)} %get-tuple-element.605) | copy-start | bytes 292
  185.3 24.1 %collective-permute-start.7 = (bf16[1560,128]{1,0:T(8,128)(2,1)}, bf16[1560,128]{1,0:T(8,128)(2,1)}, u32[]{:S(2)}, u32[]{:S(2)}) collective-permute-start(bf16[1560,128]{1,0:T(8,128)(2,1)} %pad_maximum_fusion.8), channel_id=1, source_target_pairs={{0,16},{4,20},{8,24},{12,28},{1,17},{5,21},{9,25},{13,29},{2,18},{... | collective-permute-start | bytes 1198088 | tf_op jit(solution)/shard_map/ppermute | solution.py:30
  217.0 18.1 %copy-start.16 = (f32[128,1536]{1,0:T(8,128)}, f32[128,1536]{1,0:T(8,128)S(1)}, u32[]{:S(2)}) copy-start(f32[128,1536]{1,0:T(8,128)S(1)} %copy.223) | copy-start | bytes 2359300
  235.2 19.7 %copy-start.24 = (f32[128,1024]{1,0:T(8,128)}, f32[128,1024]{1,0:T(8,128)S(1)}, u32[]{:S(2)}) copy-start(f32[128,1024]{1,0:T(8,128)S(1)} %get-tuple-element.660) | copy-start | bytes 1572868
  263.9 347.1 %reduce-scatter.5.cloned.1.call-start = ((), (), s32[]{:S(2)}) async-start(), calls=%async_computation.5 | async-start | bytes 8921088 | tf_op jit(solution)/shard_map/reduce_scatter | solution.py:536
  284.9 39.3 %collective-permute-start.8 = (bf16[4,128,256]{2,1,0:T(8,128)(2,1)}, bf16[4,128,256]{2,1,0:T(8,128)(2,1)}, u32[]{:S(2)}, u32[]{:S(2)}) collective-permute-start(bf16[4,128,256]{2,1,0:T(8,128)(2,1)} %fusion.130), channel_id=1, source_target_pairs={{0,4},{4,0},{8,12},{12,8},{16,20},{20,16},{24,28},{28,24},{1,5},{5... | collective-permute-start | bytes 786440 | tf_op jit(solution)/shard_map/ppermute | solution.py:59
  297.1 57.1 %collective-permute-start.11 = (bf16[1560,128]{1,0:T(8,128)(2,1)}, bf16[1560,128]{1,0:T(8,128)(2,1)S(1)}, u32[]{:S(2)}, u32[]{:S(2)}) collective-permute-start(bf16[1560,128]{1,0:T(8,128)(2,1)} %pad_maximum_fusion.9), channel_id=1, source_target_pairs={{4,0},{8,4},{12,8},{16,12},{20,16},{24,20},{28,24},{5,1},{9,5},{13... | collective-permute-start | bytes 1198088 | tf_op jit(solution)/shard_map/ppermute | solution.py:30
  325.6 16.9 %collective-permute-start.9 = (bf16[2,128,256]{2,1,0:T(8,128)(2,1)S(1)}, bf16[2,128,256]{2,1,0:T(8,128)(2,1)S(1)}, u32[]{:S(2)}, u32[]{:S(2)}) collective-permute-start(bf16[2,128,256]{2,1,0:T(8,128)(2,1)S(1)} %fusion.138), channel_id=1, source_target_pairs={{0,8},{4,12},{8,0},{12,4},{16,24},{20,28},{24,16},{28,20},{1,9},{5... | collective-permute-start | bytes 393224 | tf_op jit(solution)/shard_map/ppermute | solution.py:59
  342.5 17.6 %collective-permute-start.10 = (bf16[1,128,256]{2,1,0:T(8,128)(2,1)S(1)}, bf16[1,128,256]{2,1,0:T(8,128)(2,1)}, u32[]{:S(2)}, u32[]{:S(2)}) collective-permute-start(bf16[1,128,256]{2,1,0:T(8,128)(2,1)S(1)} %fusion.149), channel_id=1, source_target_pairs={{0,16},{4,20},{8,24},{12,28},{16,0},{20,4},{24,8},{28,12},{1,17},{... | collective-permute-start | bytes 196616 | tf_op jit(solution)/shard_map/ppermute | solution.py:59
  355.3 38.8 %copy-start.119 = (f32[24]{0:T(128)}, f32[24]{0:T(128)S(1)}, u32[]{:S(2)}) copy-start(f32[24]{0:T(128)S(1)} %slice_reduce_fusion.2) | copy-start | bytes 292
  356.4 16.9 %collective-permute-start.12 = (bf16[1560,128]{1,0:T(8,128)(2,1)}, bf16[1560,128]{1,0:T(8,128)(2,1)S(1)}, u32[]{:S(2)}, u32[]{:S(2)}) collective-permute-start(bf16[1560,128]{1,0:T(8,128)(2,1)} %pad_maximum_fusion.10), channel_id=1, source_target_pairs={{4,0},{8,4},{12,8},{16,12},{20,16},{24,20},{28,24},{5,1},{9,5},{13... | collective-permute-start | bytes 1198088 | tf_op jit(solution)/shard_map/ppermute | solution.py:30
  373.3 20.6 %copy-start.14 = (f32[1560,128]{1,0:T(8,128)}, f32[1560,128]{1,0:T(8,128)S(1)}, u32[]{:S(2)}) copy-start(f32[1560,128]{1,0:T(8,128)S(1)} %convert_element_type.233) | copy-start | bytes 2396164
  376.0 17.9 %collective-permute-start.13 = (bf16[1560,128]{1,0:T(8,128)(2,1)S(1)}, bf16[1560,128]{1,0:T(8,128)(2,1)S(1)}, u32[]{:S(2)}, u32[]{:S(2)}) collective-permute-start(bf16[1560,128]{1,0:T(8,128)(2,1)S(1)} %pad_maximum_fusion.11), channel_id=1, source_target_pairs={{8,0},{12,4},{16,8},{20,12},{24,16},{28,20},{9,1},{13,5},{17,9},{2... | collective-permute-start | bytes 1198088 | tf_op jit(solution)/shard_map/ppermute | solution.py:30
  400.6 25.3 %collective-permute-start.14 = (bf16[1560,128]{1,0:T(8,128)(2,1)}, bf16[1560,128]{1,0:T(8,128)(2,1)}, u32[]{:S(2)}, u32[]{:S(2)}) collective-permute-start(bf16[1560,128]{1,0:T(8,128)(2,1)} %pad_maximum_fusion.12), channel_id=1, source_target_pairs={{16,0},{20,4},{24,8},{28,12},{17,1},{21,5},{25,9},{29,13},{18,2},{... | collective-permute-start | bytes 1198088 | tf_op jit(solution)/shard_map/ppermute | solution.py:30
  404.6 22.3 %copy-start.120 = (f32[24]{0:T(128)S(1)}, f32[24]{0:T(128)}, u32[]{:S(2)}) copy-start(f32[24]{0:T(128)} %copy-done.119) | copy-start | bytes 292
  404.6 22.3 %copy-start.130 = (f32[24]{0:T(128)S(1)}, f32[24]{0:T(128)}, u32[]{:S(2)}) copy-start(f32[24]{0:T(128)} %copy-done.129) | copy-start | bytes 292
  405.6 21.4 %copy-start.128 = (f32[24]{0:T(128)S(1)}, f32[24]{0:T(128)}, u32[]{:S(2)}) copy-start(f32[24]{0:T(128)} %copy-done.127) | copy-start | bytes 292
  405.7 21.3 %copy-start.32 = (f32[1536,128]{1,0:T(8,128)S(1)}, f32[1536,128]{1,0:T(8,128)}, u32[]{:S(2)}) copy-start(f32[1536,128]{1,0:T(8,128)} %slice.390) | copy-start | bytes 2359300
  439.1 9.0 %collective-permute-start.15 = (f32[3,1792]{1,0:T(4,128)S(1)}, f32[3,1792]{1,0:T(4,128)S(1)}, u32[]{:S(2)}, u32[]{:S(2)}) collective-permute-start(f32[3,1792]{1,0:T(4,128)S(1)} %pad_add_fusion.1), channel_id=1, source_target_pairs={{4,0},{8,4},{12,8},{16,12},{20,16},{24,20},{28,24},{5,1},{9,5},{13... | collective-permute-start | bytes 64520 | tf_op jit(solution)/shard_map/ppermute | solution.py:30
  478.8 55.6 %copy-start.141 = (f32[128]{0:T(128)S(1)}, f32[128]{0:T(128)}, u32[]{:S(2)}) copy-start(f32[128]{0:T(128)} %copy-done.140) | copy-start | bytes 1540
  478.8 55.6 %copy-start.10 = (f32[128,1024]{1,0:T(8,128)S(1)}, f32[128,1024]{1,0:T(8,128)}, u32[]{:S(2)}) copy-start(f32[128,1024]{1,0:T(8,128)} %copy-done.9) | copy-start | bytes 1572868
  485.3 50.1 %copy-start.41 = (bf16[32,8192]{1,0:T(8,128)(2,1)S(1)}, bf16[32,8192]{1,0:T(8,128)(2,1)}, u32[]{:S(2)}) copy-start(bf16[32,8192]{1,0:T(8,128)(2,1)} %reduce-scatter.3.cloned.1.call-done) | copy-start | bytes 1572868
  (120 other events, 620.3 us)
Sparse Core Ops, SparseCore 0:
  12.3 81.2 all-gather.2
  97.0 134.1 all-gather.4
  264.0 199.9 reduce-scatter.2
  473.1 137.8 reduce-scatter.4
